TPU v7x, 32 devices: a whole 2x2x4 slice. The times are simulated.
32 devices in a mesh: seq: 16 (over z, x, core), wshard: 2 (over y).
Axes of the slice: x: 2, y: 2, z: 4, core: 2. Of those that a mesh axis runs over, the one named last changes fastest.
Arguments:
- hidden: bfloat16 [8, 2048, 1024], P('wshard', 'seq'), may hold values from -6 to 6
- segments: int32 [8, 2048], P('wshard', 'seq'), may hold values from 0 to 2, never falling along the last dimension, each value on 1 to 1536 neighbouring positions
- cotangent: bfloat16 [8, 2048, 1024], P('wshard', 'seq'), may hold values from -6 to 6
- in_weight: bfloat16 [1024, 3, 1024], P(None, None, 'wshard'), may hold values from -0.1875 to 0.1875
- out_weight: bfloat16 [1024, 1024], P('wshard'), may hold values from -0.1875 to 0.1875
- gate_weight: bfloat16 [1024, 4608], P(None, 'wshard'), may hold values from -0.1875 to 0.1875
- up_weight: bfloat16 [1024, 4608], P(None, 'wshard'), may hold values from -0.1875 to 0.1875
- down_weight: bfloat16 [4608, 1024], P('wshard'), may hold values from -0.09375 to 0.09375
- conv_weight: bfloat16 [3, 1024], P(None, 'wshard'), may hold values from -3 to 3
- norm_mix: bfloat16 [1024], P('wshard'), may hold values from 0.5 to 1.5
- norm_ffn: bfloat16 [1024], P('wshard'), may hold values from 0.5 to 1.5
Outputs:
- block_out: bfloat16 [8, 2048, 1024], P('wshard', 'seq')
- grad_hidden: float32 [8, 2048, 1024], P('wshard', 'seq')
- grad_in: float32 [1024, 3, 1024], P('seq', None, 'wshard')
- grad_out: float32 [1024, 1024], P('wshard', 'seq')
- grad_gate: float32 [1024, 4608], P('seq', 'wshard')
- grad_up: float32 [1024, 4608], P('seq', 'wshard')
- grad_down: float32 [4608, 1024], P('wshard', 'seq')
- grad_conv: float32 [3, 1024], P(None, 'wshard')
- grad_norm_mix: float32 [1024], P('wshard')
- grad_norm_ffn: float32 [1024], P('wshard')
Inputs may be any that keep to these rules, and one draw needn't show every extreme that they name: `segments`: segment numbers never fall along a sequence; each document holds 1 to 1536 tokens, one exactly that many.
All inputs are finite; a program needn't handle non-finite values.
Results may differ from a plain program's by a relative error of at most 0.017.
Values may be sent and summed in bfloat16 or wider, within the bound.
No kernel may reach another device: no remote copies, remote signals or barrier semaphores. Data moves between devices by JAX's collectives and lax.ppermute only.
A program may use at most 256 MiB of HBM per device.

v0:
```python
import jax
import jax.numpy as jnp
from jax import lax
from jax.sharding import PartitionSpec as P

EPS = 1e-05


def passed_along(block, axis, distance):
    devices = range(lax.axis_size(axis))
    route = [(i - distance, i) for i in devices if i - distance in devices]
    return lax.ppermute(block, axis, route)


def norm_stats(values):
    return lax.rsqrt(jnp.mean(values * values, axis=-1, keepdims=True) + EPS)


def norm_back(upstream, values, scale, gain):
    scaled = values * scale
    weighted = upstream * gain
    inner = jnp.mean(weighted * scaled, axis=-1, keepdims=True)
    return scale * (weighted - scaled * inner)


def contract_rows(left, right):
    return lax.dot_general(
        left, right, (((0,), (0,)), ((), ())), preferred_element_type=jnp.float32
    )


def contract_cols(left, right):
    return lax.dot_general(
        left, right, (((1,), (1,)), ((), ())), preferred_element_type=jnp.float32
    )


def seq_major(grad, seq_size, pair_size):
    lead_rows = grad.shape[0]
    last_cols = grad.shape[-1]
    middle = grad.shape[1:-1]
    blocked = grad.reshape(
        (seq_size, lead_rows // seq_size) + middle + (pair_size, last_cols // pair_size)
    )
    moved = jnp.moveaxis(blocked, -2, 1)
    return moved.reshape((pair_size * lead_rows,) + middle + (last_cols // pair_size,))


def pair_major(grad, seq_size, pair_size):
    row_total, col_total = grad.shape
    blocked = grad.reshape(pair_size, row_total // pair_size, seq_size, col_total // seq_size)
    return jnp.transpose(blocked, (2, 0, 1, 3)).reshape(seq_size * row_total, col_total // seq_size)


def local(
    hidden,
    segments,
    cotangent,
    in_weight,
    out_weight,
    gate_weight,
    up_weight,
    down_weight,
    conv_weight,
    norm_mix,
    norm_ffn,
):
    seq_count, seq_tokens, width = hidden.shape
    pair_size = lax.axis_size("wshard")
    pair_index = lax.axis_index("wshard")
    in_full, out_mat, gate_mat, up_mat, down_mat, taps_low, gain_mix, gain_ffn = (
        lax.all_gather(in_weight, "wshard", axis=2, tiled=True),
        lax.all_gather(out_weight, "wshard", axis=0, tiled=True),
        lax.all_gather(gate_weight, "wshard", axis=1, tiled=True),
        lax.all_gather(up_weight, "wshard", axis=1, tiled=True),
        lax.all_gather(down_weight, "wshard", axis=0, tiled=True),
        lax.all_gather(conv_weight, "wshard", axis=1, tiled=True),
        lax.all_gather(norm_mix, "wshard", axis=0, tiled=True),
        lax.all_gather(norm_ffn, "wshard", axis=0, tiled=True),
    )
    in_mat = in_full.reshape(width, -1)
    all_hidden, all_cot = (hidden, cotangent)
    seg_float = segments.astype(jnp.float32)
    group_count = all_hidden.shape[0]
    row_count = group_count * seq_tokens
    local_width = out_mat.shape[0]
    resid = all_hidden.astype(jnp.float32).reshape(row_count, width)
    scale_mix = norm_stats(resid)
    normed_mix = (resid * scale_mix * gain_mix.astype(jnp.float32)).astype(jnp.bfloat16)
    projected = jnp.dot(normed_mix, in_mat, preferred_element_type=jnp.float32)
    b_part = projected[:, :local_width]
    c_part = projected[:, local_width : 2 * local_width]
    x_part = projected[:, 2 * local_width :]
    conv_in = (b_part * x_part).astype(jnp.bfloat16).reshape(group_count, seq_tokens, local_width)
    came_rows, came_segs = (
        passed_along(
            conv_in[:, seq_tokens - 2 :, :].astype(jnp.float32).astype(jnp.bfloat16), "seq", 1
        ).astype(jnp.float32),
        passed_along(seg_float[:, seq_tokens - 2 :].astype(jnp.bfloat16), "seq", 1).astype(
            jnp.float32
        ),
    )
    ext_rows = jnp.concatenate([came_rows, conv_in.astype(jnp.float32)], axis=1)
    ext_segs = jnp.concatenate([came_segs, seg_float], axis=1)
    keep_one = (ext_segs[:, 1 : 1 + seq_tokens] == seg_float).astype(jnp.float32)[:, :, None]
    keep_two = (ext_segs[:, :seq_tokens] == seg_float).astype(jnp.float32)[:, :, None]
    lag_one = keep_one * ext_rows[:, 1 : 1 + seq_tokens]
    lag_two = keep_two * ext_rows[:, :seq_tokens]
    current = ext_rows[:, 2:]
    taps = taps_low.astype(jnp.float32)
    conv_out = (taps[2] * current + taps[1] * lag_one + taps[0] * lag_two).reshape(
        row_count, local_width
    )
    mixed = (c_part * conv_out).astype(jnp.bfloat16)
    mix_term = jnp.dot(mixed, out_mat, preferred_element_type=jnp.float32)
    resid_two = resid + mix_term
    scale_ffn = norm_stats(resid_two)
    gain_ffn_f = gain_ffn.astype(jnp.float32)
    normed_ffn = (resid_two * scale_ffn * gain_ffn_f).astype(jnp.bfloat16)
    gate = jnp.dot(normed_ffn, gate_mat, preferred_element_type=jnp.float32)
    up_value = jnp.dot(normed_ffn, up_mat, preferred_element_type=jnp.float32)
    sigma = jax.nn.sigmoid(gate)
    silu_gate = gate * sigma
    act = (silu_gate * up_value).astype(jnp.bfloat16)
    ffn_term = jnp.dot(act, down_mat, preferred_element_type=jnp.float32).reshape(
        group_count, seq_tokens, width
    )
    block_out = (resid_two.reshape(seq_count, seq_tokens, width) + ffn_term).astype(jnp.bfloat16)
    upstream = all_cot.astype(jnp.float32).reshape(row_count, width)
    upstream_low = upstream.astype(jnp.bfloat16)
    grad_down = contract_rows(act, upstream_low)
    d_act = contract_cols(upstream_low, down_mat)
    d_gate = (d_act * up_value * sigma * (1.0 + gate * (1.0 - sigma))).astype(jnp.bfloat16)
    d_up = (d_act * silu_gate).astype(jnp.bfloat16)
    grad_gate = contract_rows(normed_ffn, d_gate)
    grad_up = contract_rows(normed_ffn, d_up)
    d_normed_ffn = contract_cols(d_gate, gate_mat) + contract_cols(d_up, up_mat)
    d_resid_two = upstream + norm_back(d_normed_ffn, resid_two, scale_ffn, gain_ffn_f)
    gain_terms = d_normed_ffn * resid_two * scale_ffn
    d_resid_low = d_resid_two.astype(jnp.bfloat16)
    grad_out = contract_rows(mixed, d_resid_low)
    d_mixed = contract_cols(d_resid_low, out_mat)
    d_conv = d_mixed * c_part
    d_c = d_mixed * conv_out
    d_conv3 = d_conv.reshape(group_count, seq_tokens, local_width)
    grad_taps = jnp.stack(
        [
            jnp.sum(d_conv3 * lag_two, axis=(0, 1)),
            jnp.sum(d_conv3 * lag_one, axis=(0, 1)),
            jnp.sum(d_conv3 * current, axis=(0, 1)),
        ],
        axis=0,
    )
    term_now = taps[2] * d_conv3
    term_one = taps[1] * keep_one * d_conv3
    term_two = taps[0] * keep_two * d_conv3
    d_ext = (
        jnp.pad(term_now, ((0, 0), (2, 0), (0, 0)))
        + jnp.pad(term_one, ((0, 0), (1, 1), (0, 0)))
        + jnp.pad(term_two, ((0, 0), (0, 2), (0, 0)))
    )
    returned = passed_along(d_ext[:, :2, :].astype(jnp.bfloat16), "seq", -1).astype(jnp.float32)
    d_conv_in = (
        d_ext[:, 2:, :] + jnp.pad(returned, ((0, 0), (seq_tokens - 2, 0), (0, 0)))
    ).reshape(row_count, local_width)
    d_proj = jnp.concatenate([d_conv_in * x_part, d_c, d_conv_in * b_part], axis=1).astype(
        jnp.bfloat16
    )
    grad_in = contract_rows(normed_mix, d_proj).reshape(width, 3, local_width)
    d_normed_mix = contract_cols(d_proj, in_mat)
    resid_mine, scale_mine, d_resid_mine = (resid, scale_mix, d_resid_two)
    grad_gain_ffn = jnp.sum(gain_terms, axis=0)
    gain_mix_f = gain_mix.astype(jnp.float32)
    d_resid_mix = norm_back(d_normed_mix, resid_mine, scale_mine, gain_mix_f)
    grad_gain_mix = jnp.sum(d_normed_mix * resid_mine * scale_mine, axis=0)
    grad_hidden = (d_resid_mine + d_resid_mix).reshape(seq_count, seq_tokens, width)
    sum_taps, sum_gain_mix, sum_gain_ffn = lax.psum(
        (grad_taps, grad_gain_mix, grad_gain_ffn), ("seq", "wshard")
    )
    half_width = width // pair_size
    half_start = pair_index * half_width
    out_taps = lax.dynamic_slice_in_dim(sum_taps, half_start, half_width, 1)
    out_gain_mix = lax.dynamic_slice_in_dim(sum_gain_mix, half_start, half_width, 0)
    out_gain_ffn = lax.dynamic_slice_in_dim(sum_gain_ffn, half_start, half_width, 0)
    seq_size = lax.axis_size("seq")
    sum_in, sum_out, sum_gate, sum_up, sum_down = (
        lax.psum_scatter(
            seq_major(grad_in, seq_size, pair_size),
            ("seq", "wshard"),
            scatter_dimension=0,
            tiled=True,
        ),
        lax.psum_scatter(
            pair_major(grad_out, seq_size, pair_size),
            ("seq", "wshard"),
            scatter_dimension=0,
            tiled=True,
        ),
        lax.psum_scatter(
            seq_major(grad_gate, seq_size, pair_size),
            ("seq", "wshard"),
            scatter_dimension=0,
            tiled=True,
        ),
        lax.psum_scatter(
            seq_major(grad_up, seq_size, pair_size),
            ("seq", "wshard"),
            scatter_dimension=0,
            tiled=True,
        ),
        lax.psum_scatter(
            pair_major(grad_down, seq_size, pair_size),
            ("seq", "wshard"),
            scatter_dimension=0,
            tiled=True,
        ),
    )
    return (
        block_out,
        grad_hidden,
        sum_in,
        sum_out,
        sum_gate,
        sum_up,
        sum_down,
        out_taps,
        out_gain_mix,
        out_gain_ffn,
    )


def solution(mesh):
    return jax.shard_map(
        local,
        mesh=mesh,
        in_specs=(
            P("wshard", "seq", None),
            P("wshard", "seq"),
            P("wshard", "seq", None),
            P(None, None, "wshard"),
            P("wshard", None),
            P(None, "wshard"),
            P(None, "wshard"),
            P("wshard", None),
            P(None, "wshard"),
            P("wshard"),
            P("wshard"),
        ),
        out_specs=(
            P("wshard", "seq", None),
            P("wshard", "seq", None),
            P("seq", None, "wshard"),
            P("wshard", "seq"),
            P("seq", "wshard"),
            P("seq", "wshard"),
            P("wshard", "seq"),
            P(None, "wshard"),
            P("wshard"),
            P("wshard"),
        ),
        check_vma=False,
    )
```

profile of v0, /device:TPU:0, one launch (start us, length us, event | category | flops | bytes accessed | tf_op | source)
XLA Modules:
  0.0 1602.2 jit_solution(17035064121448482052)
XLA Ops:
  31.9 63.4 %all-gather.8.cloned.1.call-done = bf16[1024,3,1024]{0,2,1:T(8,128)(2,1)} async-done(((bf16[1024,3,512]{0,2,1:T(8,128)(2,1)}), bf16[1024,3,1024]{0,2,1:T(8,128)(2,1)}) %all-gather.8.cloned.1.call-update) | async-done | bytes 6291472 | tf_op jit(solution)/shard_map/all_gather | solution.py:72
  106.8 23.2 %all-gather.10.cloned.1.call-done = bf16[1024,1024]{1,0:T(8,128)(2,1)} async-done(((bf16[512,1024]{1,0:T(8,128)(2,1)}), bf16[1024,1024]{1,0:T(8,128)(2,1)}) %all-gather.10.cloned.1.call-update) | async-done | bytes 2097168 | tf_op jit(solution)/shard_map/all_gather | solution.py:73
  134.5 115.1 %all-gather.12.cloned.1.call-done = bf16[1024,4608]{1,0:T(8,128)(2,1)} async-done(((bf16[1024,2304]{1,0:T(8,128)(2,1)}), bf16[1024,4608]{1,0:T(8,128)(2,1)}) %all-gather.12.cloned.1.call-update) | async-done | bytes 9437200 | tf_op jit(solution)/shard_map/all_gather | solution.py:74
  249.5 12.2 fusion.43
  261.8 107.2 %all-gather.14.cloned.1.call-done = bf16[1024,4608]{1,0:T(8,128)(2,1)} async-done(((bf16[1024,2304]{1,0:T(8,128)(2,1)}), bf16[1024,4608]{1,0:T(8,128)(2,1)}) %all-gather.14.cloned.1.call-update) | async-done | bytes 9437200 | tf_op jit(solution)/shard_map/all_gather | solution.py:75
  368.9 14.8 fusion
  383.8 104.6 %all-gather.16.cloned.1.call-done = bf16[4608,1024]{1,0:T(8,128)(2,1)} async-done(((bf16[2304,1024]{1,0:T(8,128)(2,1)}), bf16[4608,1024]{1,0:T(8,128)(2,1)}) %all-gather.16.cloned.1.call-update) | async-done | bytes 9437200 | tf_op jit(solution)/shard_map/all_gather | solution.py:76
  488.4 16.1 %multiply_convert_fusion = (bf16[512,4608]{1,0:T(8,128)(2,1)}, bf16[512,4608]{1,0:T(8,128)(2,1)}) fusion(f32[512,4608]{1,0:T(8,128)} %fusion.43, f32[512,4608]{1,0:T(8,128)} %get-tuple-element.45, bf16[512,1024]{1,0:T(8,128)(2,1)S(1)} %bitcast.150, bf16[4608,1024]{1,0:T(8,128)(2,1)} %all-gather.16.cloned.1.call-done), kind=kOutput, calls=%fused_computation.8 | convolution fusion | flops 4862509056 | bytes 38797312 | tf_op jit(solution)/shard_map/dot_general | solution.py:33
  547.1 11.5 fusion.45
  558.6 22.0 %reshape.143 = f32[16,64,2,2304]{3,2,1,0:T(2,128)} reshape(f32[1024,4608]{1,0:T(8,128)} %fusion.45) | data formatting | bytes 37748736 | tf_op jit(solution)/shard_map/reshape | solution.py:42
  580.6 14.1 copy.55
  594.7 11.8 fusion.46
  606.5 22.0 %reshape.145 = f32[16,64,2,2304]{3,2,1,0:T(2,128)} reshape(f32[1024,4608]{1,0:T(8,128)} %fusion.46) | data formatting | bytes 37748736 | tf_op jit(solution)/shard_map/reshape | solution.py:42
  628.5 14.1 copy.56
  652.0 11.4 convolution_bitcast_fusion
  663.4 32.0 %copy.59 = f32[16,2,2304,64]{2,1,0,3:T(2,128)} copy(f32[16,2,2304,64]{2,3,0,1:T(8,128)} %convolution_bitcast_fusion) | data formatting | bytes 37748736 | tf_op jit(solution)/shard_map/transpose | solution.py:52
  695.5 21.2 %reshape.147 = f32[73728,64]{0,1:T(8,128)} reshape(f32[16,2,2304,64]{2,1,0,3:T(2,128)} %copy.59) | data formatting | bytes 37748736 | tf_op jit(solution)/shard_map/reshape | solution.py:52
  759.3 12.0 copy.52
  771.3 15.1 add_convert_fusion
  786.4 41.5 %all-reduce.4 = (f32[3,1024]{1,0:T(4,128)S(1)}, f32[1024]{0:T(1024)S(1)}, f32[1024]{0:T(1024)S(1)}) all-reduce(f32[3,1024]{1,0:T(4,128)S(1)} %pad_maximum_fusion.3, f32[1024]{0:T(1024)S(1)} %get-tuple-element.14, f32[1024]{0:T(1024)S(1)} %copy-done.36), channel_id=1, replica_groups=mesh['seq'=16,'wshard'=2] {'seq','wshard'}, use_global_device_ids=true, to_apply=%region_12.13 | all-reduce | flops 5120 | bytes 40960 | tf_op jit(solution)/shard_map/psum | solution.py:177
  833.3 66.3 %reduce-scatter.10.cloned.1.call-done = f32[64,2304]{1,0:T(8,128)} async-done(((f32[2048,2304]{1,0:T(8,128)}), f32[64,2304]{1,0:T(8,128)}) %reduce-scatter.10.cloned.1.call-update) | async-done | bytes 589840 | tf_op jit(solution)/shard_map/reduce_scatter | solution.py:199
  899.7 212.6 %reduce-scatter.12.cloned.1.call-done = f32[64,2304]{1,0:T(8,128)} async-done(((f32[2048,2304]{1,0:T(8,128)}), f32[64,2304]{1,0:T(8,128)}) %reduce-scatter.12.cloned.1.call-update) | async-done | bytes 589840 | tf_op jit(solution)/shard_map/reduce_scatter | solution.py:205
  1112.3 211.0 %reduce-scatter.14.cloned.1.call-done = f32[2304,64]{0,1:T(8,128)} async-done(((f32[73728,64]{0,1:T(8,128)}), f32[2304,64]{0,1:T(8,128)}) %reduce-scatter.14.cloned.1.call-update) | async-done | bytes 589840 | tf_op jit(solution)/shard_map/reduce_scatter | solution.py:211
  1323.3 271.9 %reduce-scatter.6.cloned.1.call-done = f32[64,3,512]{2,0,1:T(8,128)} async-done(((f32[2048,3,512]{2,0,1:T(8,128)}), f32[64,3,512]{2,0,1:T(8,128)}) %reduce-scatter.6.cloned.1.call-update) | async-done | bytes 393232 | tf_op jit(solution)/shard_map/reduce_scatter | solution.py:187
  (170 shorter events, 140.1 us)
Async XLA Ops:
  7.2 88.1 %all-gather.8.cloned.1.call-start = ((), (), s32[]{:S(2)}) async-start(), calls=%async_computation.5 | async-start | bytes 9437184 | tf_op jit(solution)/shard_map/all_gather | solution.py:72
  11.9 118.0 %all-gather.10.cloned.1.call-start = ((), (), s32[]{:S(2)}) async-start(), calls=%async_computation.6 | async-start | bytes 3145728 | tf_op jit(solution)/shard_map/all_gather | solution.py:73
  12.7 236.8 %all-gather.12.cloned.1.call-start = ((), (), s32[]{:S(2)}) async-start(), calls=%async_computation.7 | async-start | bytes 14155776 | tf_op jit(solution)/shard_map/all_gather | solution.py:74
  13.4 355.5 %all-gather.14.cloned.1.call-start = ((), (), s32[]{:S(2)}) async-start(), calls=%async_computation.8 | async-start | bytes 14155776 | tf_op jit(solution)/shard_map/all_gather | solution.py:75
  14.0 12.1 copy-start.35
  14.0 16.6 %copy-start.4 = (bf16[4,128,1024]{2,1,0:T(8,128)(2,1)S(1)}, bf16[4,128,1024]{2,1,0:T(8,128)(2,1)}, u32[]{:S(2)}) copy-start(bf16[4,128,1024]{2,1,0:T(8,128)(2,1)} %param.11) | copy-start | bytes 3145732
  14.0 474.3 %all-gather.16.cloned.1.call-start = ((), (), s32[]{:S(2)}) async-start(), calls=%async_computation.9 | async-start | bytes 14155776 | tf_op jit(solution)/shard_map/all_gather | solution.py:76
  14.6 818.7 %reduce-scatter.8.cloned.1.call-start = ((), (), s32[]{:S(2)}) async-start(), calls=%async_computation.11 | async-start | bytes 4325376 | tf_op jit(solution)/shard_map/reduce_scatter | solution.py:193
  14.8 17.1 %collective-permute-start = (bf16[4,2]{1,0:T(4,128)(2,1)S(1)}, bf16[4,2]{1,0:T(4,128)(2,1)S(1)}, u32[]{:S(2)}, u32[]{:S(2)}) collective-permute-start(bf16[4,2]{1,0:T(4,128)(2,1)S(1)} %slice.52), channel_id=1, source_target_pairs={{0,2},{2,4},{4,6},{6,8},{8,10},{10,12},{12,14},{14,16},{16,18},{18... | collective-permute-start | bytes 56 | tf_op jit(solution)/shard_map/ppermute | solution.py:12
  21.8 9.7 copy-start.22
  31.5 72.6 %copy-start.24 = (f32[1,1024]{1,0:T(1,128)}, f32[1,1024]{1,0:T(1,128)S(1)}, u32[]{:S(2)}) copy-start(f32[1,1024]{1,0:T(1,128)S(1)} %get-tuple-element.30) | copy-start | bytes 12292
  31.5 72.6 %copy-start.26 = (f32[1,1024]{1,0:T(1,128)}, f32[1,1024]{1,0:T(1,128)S(1)}, u32[]{:S(2)}) copy-start(f32[1,1024]{1,0:T(1,128)S(1)} %get-tuple-element.31) | copy-start | bytes 12292
  31.5 72.6 %copy-start.28 = (f32[1,1024]{1,0:T(1,128)}, f32[1,1024]{1,0:T(1,128)S(1)}, u32[]{:S(2)}) copy-start(f32[1,1024]{1,0:T(1,128)S(1)} %get-tuple-element.32) | copy-start | bytes 12292
  101.4 2.6 collective-permute-start.1
  106.8 26.1 %copy-start.8 = (bf16[512,1024]{1,0:T(8,128)(2,1)}, bf16[512,1024]{1,0:T(8,128)(2,1)S(1)}, u32[]{:S(2)}) copy-start(bf16[512,1024]{1,0:T(8,128)(2,1)S(1)} %fusion.11) | copy-start | bytes 3145732
  261.7 226.6 %copy-start.13 = (bf16[4,128,1024]{2,1,0:T(8,128)(2,1)S(1)}, bf16[4,128,1024]{2,1,0:T(8,128)(2,1)}, u32[]{:S(2)}) copy-start(bf16[4,128,1024]{2,1,0:T(8,128)(2,1)} %param.13) | copy-start | bytes 3145732
  504.5 9.2 copy-start.7
  504.5 9.2 copy-start.10
  547.1 352.6 %reduce-scatter.10.cloned.1.call-start = ((), (), s32[]{:S(2)}) async-start(), calls=%async_computation.12 | async-start | bytes 19464192 | tf_op jit(solution)/shard_map/reduce_scatter | solution.py:199
  594.7 517.6 %reduce-scatter.12.cloned.1.call-start = ((), (), s32[]{:S(2)}) async-start(), calls=%async_computation.13 | async-start | bytes 19464192 | tf_op jit(solution)/shard_map/reduce_scatter | solution.py:205
  642.7 680.6 %reduce-scatter.14.cloned.1.call-start = ((), (), s32[]{:S(2)}) async-start(), calls=%async_computation.14 | async-start | bytes 19464192 | tf_op jit(solution)/shard_map/reduce_scatter | solution.py:211
  716.7 878.5 %reduce-scatter.6.cloned.1.call-start = ((), (), s32[]{:S(2)}) async-start(), calls=%async_computation.10 | async-start | bytes 12976128 | tf_op jit(solution)/shard_map/reduce_scatter | solution.py:187
  724.4 3.2 collective-permute-start.2
  771.3 15.1 copy-start.36
  (33 other events, 121.4 us)
Sparse Core Ops, SparseCore 0:
  12.0 83.1 all-gather.7
  96.8 33.1 all-gather.9
  131.5 117.9 all-gather.11
  250.9 117.9 all-gather.13
  370.3 117.9 all-gather.15
  547.2 141.5 reduce-scatter.7
  695.8 203.8 reduce-scatter.9
  906.7 205.5 reduce-scatter.11
  1119.3 203.9 reduce-scatter.13
  1326.0 269.1 reduce-scatter.5
where the time goes:
time: 1610 us; the launch traced here: 1600 us
  waiting for transfers between devices  1180 us (73%)
  local copies, waits for them, and re-layouts  189 us (12%)
  matrix products  144 us (9%)
  blocking collectives  54.9 us (3%)
    reduce_scatter x1, waiting for transfers between devices, local(): lax.psum_scatter(seq_major(grad_in, seq_size, pair_size), ('seq', 'wshard...  272 us
    reduce_scatter x1, waiting for transfers between devices, local(): lax.psum_scatter(seq_major(grad_up, seq_size, pair_size), ('seq', 'wshard...  213 us
    reduce_scatter x1, waiting for transfers between devices, local(): lax.psum_scatter(pair_major(grad_down, seq_size, pair_size), ('seq', 'wsh...  211 us
    all_gather x1, waiting for transfers between devices, local(): lax.all_gather(gate_weight, 'wshard', axis=1, tiled=True)  115 us
    all_gather x1, waiting for transfers between devices, local(): lax.all_gather(up_weight, 'wshard', axis=1, tiled=True)  107 us
    all_gather x1, waiting for transfers between devices, local(): lax.all_gather(down_weight, 'wshard', axis=0, tiled=True)  105 us
    reduce_scatter x1, waiting for transfers between devices, local(): lax.psum_scatter(seq_major(grad_gate, seq_size, pair_size), ('seq', 'wsha...  66.3 us
    all_gather x1, waiting for transfers between devices, local(): lax.all_gather(in_weight, 'wshard', axis=2, tiled=True)  63.4 us
  transfers between devices with their start and end apart: 13, of which 11 were waited for; matrix products, arithmetic and copies ran while one was open for 17% of the time, Pallas kernels for 0%

commit v1 on v0

v1 whole, which is shorter than its diff:
```python
import jax
import jax.numpy as jnp
from jax import lax
from jax.sharding import PartitionSpec as P

EPS = 1e-05
LOW = jnp.bfloat16
F32 = jnp.float32


def over_seq(block, route):
    return lax.ppermute(block, "seq", route)


def swap_seq(block, mask):
    return over_seq(block, [(i, i ^ mask) for i in range(lax.axis_size("seq"))])


def swap_core(block):
    return swap_seq(block, 1)


def swap_pair(block):
    return lax.ppermute(block, "wshard", [(0, 1), (1, 0)])


def swap(block, link):
    return swap_pair(block) if link == "pair" else swap_seq(block, 2 * link)


def mm(left, right):
    return jnp.dot(left, right, preferred_element_type=F32)


def mm_tn(left, right):
    return lax.dot_general(left, right, (((0,), (0,)), ((), ())), preferred_element_type=F32)


def mm_nt(left, right):
    return lax.dot_general(left, right, (((1,), (1,)), ((), ())), preferred_element_type=F32)


def norm_stats(values):
    return lax.rsqrt(jnp.mean(values * values, axis=-1, keepdims=True) + EPS)


def norm_back(upstream, values, scale, gain):
    scaled = values * scale
    weighted = upstream * gain
    inner = jnp.mean(weighted * scaled, axis=-1, keepdims=True)
    return scale * (weighted - scaled * inner)


def slot_masks(order):
    masks = [0]
    for link in reversed(order):
        masks = masks + [mask ^ link for mask in masks]
    return masks


def in_slots(grad, chip, order):
    chips = lax.axis_size("seq") // 2
    blocks = grad.astype(LOW).reshape(chips, grad.shape[0] // chips, grad.shape[1])
    return jnp.stack(
        [lax.dynamic_index_in_dim(blocks, chip ^ mask, 0, False) for mask in slot_masks(order)]
    )


def halving(send, keep, order):
    terms = [keep]
    half = keep.shape[0]
    terms.append(swap(send, order[0]))
    for link in order[1:]:
        half //= 2
        going = sum(term[half : 2 * half].astype(F32) for term in terms).astype(LOW)
        terms.append(swap(going, link))
    return sum(term[0].astype(F32) for term in terms)


def scatter_seq(grad, chip, order):
    slots = in_slots(grad, chip, order)
    half = slots.shape[0] // 2
    return halving(slots[half:], slots[:half], order)


def scatter_all(mine, other, chip, order):
    return halving(in_slots(other, chip, order[1:]), in_slots(mine, chip, order[1:]), order)


def local(
    hidden,
    segments,
    cotangent,
    in_weight,
    out_weight,
    gate_weight,
    up_weight,
    down_weight,
    conv_weight,
    norm_mix,
    norm_ffn,
):
    groups, block, width = hidden.shape
    rows = groups * block
    size = lax.axis_size("seq")
    seq_index = lax.axis_index("seq")
    core = seq_index % 2
    chip = seq_index // 2
    pair = lax.axis_index("wshard")
    first_core = core == 0
    chips = size // 2
    links = [1 << bit for bit in range(chips.bit_length() - 1)]
    features = out_weight.shape[0] // 2
    units = gate_weight.shape[1] // 2

    def ordered(flag, mine, other, axis):
        return jnp.where(
            flag,
            jnp.concatenate([mine, other], axis=axis),
            jnp.concatenate([other, mine], axis=axis),
        )

    small = jnp.concatenate([conv_weight, norm_mix[None], norm_ffn[None]], axis=0)
    small_other = swap_pair(small)
    gains = ordered(pair == 0, small[3:], small_other[3:], 1).astype(F32)
    gain_mix, gain_ffn = gains[0], gains[1]

    def of_core(array, axis):
        return lax.dynamic_slice_in_dim(array, core * (array.shape[axis] // 2), array.shape[axis] // 2, axis)

    taps = jnp.concatenate([of_core(small[:3], 1), of_core(small_other[:3], 1)], axis=1).astype(F32)

    in_mine = of_core(jnp.transpose(in_weight, (1, 0, 2)), 2)
    in_other = swap_pair(in_mine)
    out_mine = of_core(out_weight, 0)
    out_other = swap_pair(out_mine)
    in_mat = jnp.concatenate(
        [part for j in range(3) for part in (in_mine[j], in_other[j])], axis=1
    )
    out_mat = jnp.concatenate([out_mine, out_other], axis=0)
    conv_width = 2 * features

    own = hidden.reshape(rows, width)
    chip_hidden = jnp.concatenate([own, swap_core(own)], axis=0)
    seg_low = segments.astype(LOW)
    seg_other = swap_core(segments)

    edge = jnp.concatenate(
        [hidden, jnp.broadcast_to(seg_low[:, :, None], (groups, block, 128))], axis=2
    )
    last, head = edge[:, block - 2 :], edge[:, :2]
    odd = range(1, size - 1, 2)
    even = range(2, size, 2)
    before = jnp.where(
        first_core,
        over_seq(last, [(i, i + 1) for i in odd]),
        over_seq(last, [(i, i + 2) for i in odd]),
    )
    after = jnp.where(
        first_core,
        over_seq(head, [(i, i - 2) for i in even]),
        over_seq(head, [(i, i - 1) for i in even]),
    )
    edges = jnp.concatenate([before, after], axis=0)
    edge_hidden = edges[:, :, :width].reshape(4 * groups, width)
    edge_segs = edges[:, :, width].astype(jnp.int32)

    resid = chip_hidden.astype(F32)
    scale_mix = norm_stats(resid)
    normed_mix = (resid * scale_mix * gain_mix).astype(LOW)
    edge_resid = edge_hidden.astype(F32)
    edge_normed = (edge_resid * norm_stats(edge_resid) * gain_mix).astype(LOW)
    projected = mm(normed_mix, in_mat)
    edge_projected = mm(edge_normed, in_mat)
    b_part = projected[:, :conv_width]
    c_part = projected[:, conv_width : 2 * conv_width]
    x_part = projected[:, 2 * conv_width :]

    def by_core(array):
        return array.reshape((2, groups, block) + array.shape[1:])

    def lead(own_lead, other_lead):
        return jnp.stack([own_lead, other_lead])

    conv_in = by_core((b_part * x_part).astype(LOW).astype(F32))
    edge_conv_in = (
        (edge_projected[: 2 * groups, :conv_width] * edge_projected[: 2 * groups, 2 * conv_width :])
        .astype(LOW)
        .astype(F32)
        .reshape(groups, 2, conv_width)
    )
    edge_c = edge_projected[2 * groups :, conv_width : 2 * conv_width]
    segs = jnp.stack([segments, seg_other])
    segs_before, segs_after = edge_segs[:groups], edge_segs[groups:]

    def with_before(values, outside):
        ahead = jnp.where(
            first_core,
            lead(outside, values[0, :, block - 2 :]),
            lead(values[1, :, block - 2 :], outside),
        )
        return jnp.concatenate([ahead, values], axis=2)

    def with_after(values, outside):
        behind = jnp.where(
            first_core, lead(values[1, :, :2], outside), lead(outside, values[0, :, :2])
        )
        return jnp.concatenate([values, behind], axis=2)

    ext = with_before(conv_in, edge_conv_in)
    segs_ext = with_before(segs, segs_before)
    keep_one = (segs_ext[:, :, 1 : 1 + block] == segs).astype(F32)[..., None]
    keep_two = (segs_ext[:, :, :block] == segs).astype(F32)[..., None]
    lag_one = keep_one * ext[:, :, 1 : 1 + block]
    lag_two = keep_two * ext[:, :, :block]
    conv_out = (taps[2] * conv_in + taps[1] * lag_one + taps[0] * lag_two).reshape(2 * rows, conv_width)
    mixed = (c_part * conv_out).astype(LOW)
    mix_part = mm(mixed, out_mat).astype(LOW)
    mix_other = swap_core(mix_part)
    mix_term = mix_part.astype(F32) + jnp.concatenate([mix_other[rows:], mix_other[:rows]], axis=0).astype(F32)
    resid_two = resid + mix_term
    scale_ffn = norm_stats(resid_two)
    normed_ffn = (resid_two * scale_ffn * gain_ffn).astype(LOW)

    def gathered(mine):
        far = swap_pair(mine)
        return far, swap_core(far)

    cot = cotangent.reshape(rows, width)
    cot_chip = jnp.concatenate([cot, swap_core(cot)], axis=0)
    cot_far = jnp.concatenate(gathered(cot), axis=0)
    normed_far = jnp.concatenate(gathered(normed_ffn[:rows]), axis=0)
    gate_mat = of_core(gate_weight, 1)
    up_mat = of_core(up_weight, 1)
    down_mat = of_core(down_weight, 0)

    def feed_forward(normed, upstream):
        gate = mm(normed, gate_mat)
        up_value = mm(normed, up_mat)
        d_act = mm_nt(upstream, down_mat)
        sigma = jax.nn.sigmoid(gate)
        silu_gate = gate * sigma
        act = (silu_gate * up_value).astype(LOW)
        d_gate = (d_act * up_value * sigma * (1.0 + gate * (1.0 - sigma))).astype(LOW)
        d_up = (d_act * silu_gate).astype(LOW)
        term = mm(act, down_mat).astype(LOW)
        d_normed = (mm_nt(d_gate, gate_mat) + mm_nt(d_up, up_mat)).astype(LOW)
        return act, d_gate, d_up, term, d_normed

    near_out = feed_forward(normed_ffn, cot_chip)
    far_out = feed_forward(normed_far, cot_far)

    def home(near, far):
        near_sum = near[:rows].astype(F32) + swap_core(near[rows:]).astype(F32)
        far_sum = (far[:rows].astype(F32) + swap_core(far[rows:]).astype(F32)).astype(LOW)
        return near_sum + swap_pair(far_sum).astype(F32)

    d_normed_ffn = home(near_out[4], far_out[4])
    block_out = (resid_two[:rows] + home(near_out[3], far_out[3])).astype(LOW)

    all_normed = jnp.concatenate([normed_ffn, normed_far], axis=0)
    all_cot = jnp.concatenate([cot_chip, cot_far], axis=0)
    act, d_gate, d_up = (jnp.concatenate([near_out[i], far_out[i]], axis=0) for i in range(3))
    part_down = scatter_seq(mm_tn(all_cot, act), chip, links)
    part_gate = scatter_seq(mm_tn(all_normed, d_gate), chip, links)
    part_up = scatter_seq(mm_tn(all_normed, d_up), chip, links)

    upstream = cot.astype(F32)
    own_two, own_scale = resid_two[:rows], scale_ffn[:rows]
    d_resid_two = upstream + norm_back(d_normed_ffn, own_two, own_scale, gain_ffn)
    grad_gain_ffn = jnp.sum(d_normed_ffn * own_two * own_scale, axis=0)
    d_resid_low = d_resid_two.astype(LOW)
    d_chip = jnp.concatenate([d_resid_low, swap_core(d_resid_low)], axis=0)
    d_head = d_resid_low.reshape(groups, block, width)[:, :2]
    d_after = jnp.where(
        first_core,
        over_seq(d_head, [(i, i - 2) for i in even]),
        over_seq(d_head, [(i, i - 1) for i in even]),
    ).reshape(2 * groups, width)
    d_mixed = mm_nt(d_chip, out_mat)
    edge_d_conv = (mm_nt(d_after, out_mat) * edge_c).reshape(groups, 2, conv_width)
    d_conv = by_core(d_mixed * c_part)
    d_c = d_mixed * conv_out
    grad_taps = jnp.stack(
        [
            jnp.sum(d_conv * lag_two, axis=(0, 1, 2)),
            jnp.sum(d_conv * lag_one, axis=(0, 1, 2)),
            jnp.sum(d_conv * conv_in, axis=(0, 1, 2)),
        ]
    )
    d_ext = with_after(d_conv, edge_d_conv)
    segs_next = with_after(segs, segs_after)
    next_one = (segs_next[:, :, 1 : 1 + block] == segs).astype(F32)[..., None]
    next_two = (segs_next[:, :, 2 : 2 + block] == segs).astype(F32)[..., None]
    d_conv_in = (
        taps[2] * d_conv
        + taps[1] * next_one * d_ext[:, :, 1 : 1 + block]
        + taps[0] * next_two * d_ext[:, :, 2 : 2 + block]
    ).reshape(2 * rows, conv_width)
    d_proj = jnp.concatenate([d_conv_in * x_part, d_c, d_conv_in * b_part], axis=1).astype(LOW)
    grad_out = mm_tn(d_chip, mixed)
    grad_in = mm_tn(normed_mix, d_proj)
    d_normed_part = mm_nt(d_proj, in_mat).astype(LOW)
    d_normed_mix = d_normed_part[:rows].astype(F32) + swap_core(d_normed_part[rows:]).astype(F32)
    own_resid, own_mix = resid[:rows], scale_mix[:rows]
    grad_hidden = (d_resid_two + norm_back(d_normed_mix, own_resid, own_mix, gain_mix)).reshape(
        groups, block, width
    )
    grad_gain_mix = jnp.sum(d_normed_mix * own_resid * own_mix, axis=0)

    halves = [grad_out] + [grad_in[:, j * conv_width : (j + 1) * conv_width] for j in range(3)]
    mixed_mine = jnp.concatenate([half[:, :features] for half in halves], axis=1)
    mixed_far = jnp.concatenate([half[:, features:] for half in halves], axis=1)
    part_mix = scatter_all(mixed_mine, mixed_far, chip, ["pair"] + links)

    part_rows = width // size

    def finish(part):
        low = part.astype(LOW).reshape(2, part_rows, -1)
        came = swap_core(lax.dynamic_index_in_dim(low, 1 - core, 0, False)).astype(F32)
        mine = lax.dynamic_index_in_dim(part.reshape(2, part_rows, -1), core, 0, False)
        return mine, came

    def wide(part):
        mine, came = finish(part)
        return ordered(first_core, mine, came, 1)

    out_down = wide(part_down).T
    out_gate = wide(part_gate)
    out_up = wide(part_up)
    mix_mine, mix_came = finish(part_mix)
    mix_parts = [
        ordered(
            first_core,
            mix_mine[:, j * features : (j + 1) * features],
            mix_came[:, j * features : (j + 1) * features],
            1,
        )
        for j in range(4)
    ]
    out_out = mix_parts[0].T
    out_in = jnp.stack(mix_parts[1:], axis=1)

    half_width = norm_mix.shape[0]
    spread = jnp.zeros((3, width), F32)
    spread = lax.dynamic_update_slice_in_dim(
        spread, grad_taps[:, :features], pair * half_width + core * features, 1
    )
    spread = lax.dynamic_update_slice_in_dim(
        spread, grad_taps[:, features:], (1 - pair) * half_width + core * features, 1
    )
    sums = lax.psum(
        jnp.concatenate([spread, grad_gain_mix[None], grad_gain_ffn[None]], axis=0), ("seq", "wshard")
    )
    sums = lax.dynamic_slice_in_dim(sums, pair * half_width, half_width, 1)
    return (
        block_out.reshape(groups, block, width),
        grad_hidden,
        out_in,
        out_out,
        out_gate,
        out_up,
        out_down,
        sums[:3],
        sums[3],
        sums[4],
    )


def solution(mesh):
    return jax.shard_map(
        local,
        mesh=mesh,
        in_specs=(
            P("wshard", "seq", None),
            P("wshard", "seq"),
            P("wshard", "seq", None),
            P(None, None, "wshard"),
            P("wshard", None),
            P(None, "wshard"),
            P(None, "wshard"),
            P("wshard", None),
            P(None, "wshard"),
            P("wshard"),
            P("wshard"),
        ),
        out_specs=(
            P("wshard", "seq", None),
            P("wshard", "seq", None),
            P("seq", None, "wshard"),
            P("wshard", "seq"),
            P("seq", "wshard"),
            P("seq", "wshard"),
            P("wshard", "seq"),
            P(None, "wshard"),
            P("wshard"),
            P("wshard"),
        ),
        check_vma=False,
    )
```

time: 1610 us -> 524 us (0.33)
  waiting for transfers between devices: 1180 us -> 232 us
  local copies, waits for them, and re-layouts: 189 us -> 39 us
  other arithmetic: 14.2 us -> 45.7 us
  starting transfers between devices: 5.91 us -> 36 us
  matrix products: 144 us -> 123 us
    reduce_scatter x5 -> x0, waiting for transfers between devices: 762 us -> none  [the longest x1 272 us: local(): lax.psum_scatter(seq_major(grad_in, seq_size, pair_size), ('seq', 'wshard...]
    all_gather x5 -> x0, waiting for transfers between devices: 413 us -> none  [the longest x1 115 us: local(): lax.all_gather(gate_weight, 'wshard', axis=1, tiled=True)]
    ppermute x3 -> x42, waiting for transfers between devices: 1.64 us -> 232 us  [the longest x34 144 us: over_seq(): return lax.ppermute(block, 'seq', route)]
    transpose x5 -> x0, local copies, waits for them, and re-layouts: 78.8 us -> none  [the longest x3 40.2 us: seq_major(): moved = jnp.moveaxis(blocked, -2, 1)]
    reshape x5 -> x1, local copies, waits for them, and re-layouts: 78.4 us -> 0.01 us  [local(): d_after = jnp.where(first_core, over_seq(d_head, [(i, i - 2) for i in eve...]
    ppermute x3 -> x42, starting transfers between devices: 5.51 us -> 36 us  [the longest x34 26.2 us: over_seq(): return lax.ppermute(block, 'seq', route)]
    dot_general x15 -> x23, matrix products: 144 us -> 123 us  [the longest x9 50.3 us: mm_nt(): lax.dot_general(left, right, (((1,), (1,)), ((), ())), preferred_element_...]
    convert_element_type x9 -> x26, other arithmetic: 1.64 us -> 22 us  [the longest x9 5.75 us: halving(): going = sum((term[half:2 * half].astype(F32) for term in terms)).astype(LOW)]
  transfers between devices with their start and end apart: 13 -> 42, of which waited for: 11 -> 15; matrix products, arithmetic and copies ran while one was open for 17% -> 33% of each run, Pallas kernels for 0% -> 0%
where the time goes in v1:
time: 524 us; the launch traced here: 518 us
  waiting for transfers between devices  232 us (44%)
  matrix products  123 us (23%)
  other arithmetic  45.7 us (9%)
  blocking collectives  40.1 us (8%)
  local copies, waits for them, and re-layouts  39 us (7%)
  starting transfers between devices  36 us (7%)
    ppermute x34, waiting for transfers between devices, over_seq(): return lax.ppermute(block, 'seq', route)  144 us
    ppermute x8, waiting for transfers between devices, swap_pair(): return lax.ppermute(block, 'wshard', [(0, 1), (1, 0)])  88.6 us
    dot_general x9, matrix products, mm_nt(): lax.dot_general(left, right, (((1,), (1,)), ((), ())), preferred_element_...  50.3 us
    psum x1, blocking collectives, local(): lax.psum(jnp.concatenate([spread, grad_gain_mix[None], grad_gain_ffn[None...  40.1 us
    dot_general x9, matrix products, mm(): return jnp.dot(left, right, preferred_element_type=F32)  39.4 us
    dot_general x5, matrix products, mm_tn(): lax.dot_general(left, right, (((0,), (0,)), ((), ())), preferred_element_...  32.9 us
    ppermute x34, starting transfers between devices, over_seq(): return lax.ppermute(block, 'seq', route)  26.2 us
    unnamed x125, local copies, waits for them, and re-layouts  18.8 us
  transfers between devices with their start and end apart: 42, of which 15 were waited for; matrix products, arithmetic and copies ran while one was open for 33% of the time, Pallas kernels for 0%

profile of v1, /device:TPU:0, one launch (start us, length us, event | category | flops | bytes accessed | tf_op | source)
XLA Modules:
  0.0 517.6 jit_solution(11000948463357092600)
XLA Ops:
  12.7 4.7 collective-permute-start.7
  21.6 25.2 %collective-permute-done.1 = bf16[5,512]{1,0:T(8,128)(2,1)S(1)} collective-permute-done((bf16[5,512]{1,0:T(8,128)(2,1)S(1)}, bf16[5,512]{1,0:T(8,128)(2,1)S(1)}, u32[]{:S(2)}, u32[]{:S(2)}) %collective-permute-start.1) | collective-permute-done | bytes 5152 | tf_op jit(solution)/shard_map/ppermute | solution.py:24
  63.7 5.4 %fusion.73 = f32[1024,1536]{1,0:T(8,128)S(1)} fusion(bf16[1024,1536]{1,0:T(8,128)(2,1)} %fusion.75, f32[1024]{0:T(1024)S(1)} %bitcast.190, f32[1024]{0:T(1024)S(1)} %add_rsqrt_fusion.1, bf16[512,1024]{1,0:T(8,128)(2,1)S(1)} %collective-permute-done, bf16[512,1024]{1,0:T(8,128)(2,1)S(1)} %bitcast.148), kind=kOutput, calls=%fused_computation.131 | convolution fusion | flops 3228565504 | bytes 11542528 | tf_op jit(solution)/shard_map/dot_general | solution.py:32
  79.7 23.4 %collective-permute-done.17 = bf16[512,1024]{1,0:T(8,128)(2,1)} collective-permute-done((bf16[512,1024]{1,0:T(8,128)(2,1)}, bf16[512,1024]{1,0:T(8,128)(2,1)}, u32[]{:S(2)}, u32[]{:S(2)}) %collective-permute-start.17) | collective-permute-done | bytes 1048608 | tf_op jit(solution)/shard_map/ppermute | solution.py:24
  122.6 9.7 %multiply_convert_fusion.2 = (bf16[1024,1152]{1,0:T(8,128)(2,1)S(1)}, bf16[1024,1152]{1,0:T(8,128)(2,1)}, bf16[1024,1152]{1,0:T(8,128)(2,1)}) fusion(f32[1024,1152]{1,0:T(8,128)} %fusion.69, f32[1024,1152]{1,0:T(8,128)} %fusion.61, bf16[2304,1024]{1,0:T(8,128)(2,1)S(1)} %bitcast.220, s32[]{:T(128)S(6)} %select_n.227, ...), kind=kOutput, calls=%fused_computation.14 | convolution fusion | flops 2437808128 | bytes 20971524 | tf_op jit(solution)/shard_map/dot_general | solution.py:40
  132.3 6.1 %fusion.65 = f32[1024,1024]{1,0:T(8,128)S(1)} fusion(bf16[1024,1152]{1,0:T(8,128)(2,1)} %get-tuple-element.24, bf16[1024,2304]{1,0:T(8,128)(2,1)} %param.16, s32[]{:T(128)S(6)} %select_n.227), kind=kOutput, calls=%fused_computation.113 | convolution fusion | flops 2415919104 | bytes 8912900 | tf_op jit(solution)/shard_map/dot_general | solution.py:40
  138.8 5.0 add_convert_fusion.1
  158.7 11.4 %multiply_convert_fusion = (bf16[1024,1152]{1,0:T(8,128)(2,1)S(1)}, bf16[1024,1152]{1,0:T(8,128)(2,1)}, bf16[1024,1152]{1,0:T(8,128)(2,1)}) fusion(f32[1024,1152]{1,0:T(8,128)} %fusion.67, f32[1024,1152]{1,0:T(8,128)} %fusion.59, bf16[2304,1024]{1,0:T(8,128)(2,1)} %param.18, s32[]{:T(128)S(6)} %select_n.227, bf16[512,1024]{1,0:T(8,128)(2,1)} %collective-permute-done.18, ...), kind=kOutput, calls=%fused_computation.12 | convolution fusion | flops 2437808128 | bytes 20971524 | tf_op jit(solution)/shard_map/dot_general | solution.py:40
  170.1 6.1 %convolution_convert_fusion.1 = bf16[1024,1024]{1,0:T(8,128)(2,1)S(1)} fusion(bf16[1024,1152]{1,0:T(8,128)(2,1)} %get-tuple-element.28, bf16[2304,1024]{1,0:T(8,128)(2,1)} %param.18, s32[]{:T(128)S(6)} %select_n.227), kind=kOutput, calls=%fused_computation.96 | convolution fusion | flops 2416967680 | bytes 6815748 | tf_op jit(solution)/shard_map/dot_general | solution.py:32
  187.8 9.3 %fusion.21 = bf16[1024,1152]{1,0:T(8,128)(2,1)S(1)} fusion(bf16[1024,1152]{1,0:T(8,128)(2,1)} %get-tuple-element.28, bf16[1024,1152]{1,0:T(8,128)(2,1)} %get-tuple-element.25, bf16[512,1024]{1,0:T(8,128)(2,1)} %collective-permute-done.18, bf16[512,1024]{1,0:T(8,128)(2,1)} %collective-permute-done.17, bf16[512,1024]{1,0:T(8,128)(2,1)} %collective-permute-done.15, ...), kind=kOutput, calls=%fused_computation.37 | convolution fusion | flops 4859232256 | bytes 11272192 | tf_op jit(solution)/shard_map/dot_general | solution.py:36
  200.0 8.2 %fusion.26 = bf16[1024,1152]{1,0:T(8,128)(2,1)S(1)} fusion(bf16[1024,1152]{1,0:T(8,128)(2,1)} %copy-done.38, bf16[1024,1152]{1,0:T(8,128)(2,1)} %copy-done.37, bf16[512,1024]{1,0:T(8,128)(2,1)S(1)} %collective-permute-done.12, bf16[512,1024]{1,0:T(8,128)(2,1)S(1)} %collective-permute-done.11, bf16[1024,1024]{1,0:T(8,128)(2,1)S(1)} %multiply_convert_fusion.6), kind=kOutput, calls=%fused_computation.38 | convolution fusion | flops 4855037952 | bytes 11272192 | tf_op jit(solution)/shard_map/dot_general | solution.py:36
  210.3 8.8 %fusion.29 = bf16[1024,1152]{1,0:T(8,128)(2,1)S(1)} fusion(bf16[1024,1152]{1,0:T(8,128)(2,1)} %get-tuple-element.27, bf16[1024,1152]{1,0:T(8,128)(2,1)} %get-tuple-element.24, bf16[512,1024]{1,0:T(8,128)(2,1)} %copy-done.24, bf16[512,1024]{1,0:T(8,128)(2,1)} %copy-done.23, bf16[1024,1024]{1,0:T(8,128)(2,1)S(1)} %multiply_convert_fusion.6), kind=kOutput, calls=%fused_computation.39 | convolution fusion | flops 4855037952 | bytes 11272192 | tf_op jit(solution)/shard_map/dot_general | solution.py:36
  229.4 23.4 %collective-permute-done.34 = bf16[4,128,1152]{2,1,0:T(8,128)(2,1)} collective-permute-done((bf16[4,128,1152]{2,1,0:T(8,128)(2,1)}, bf16[4,128,1152]{2,1,0:T(8,128)(2,1)}, u32[]{:S(2)}, u32[]{:S(2)}) %collective-permute-start.34) | collective-permute-done | bytes 1179680 | tf_op jit(solution)/shard_map/ppermute | solution.py:12
  255.7 21.7 %collective-permute-done.30 = bf16[4,128,1152]{2,1,0:T(8,128)(2,1)S(1)} collective-permute-done((bf16[4,128,1152]{2,1,0:T(8,128)(2,1)S(1)}, bf16[4,128,1152]{2,1,0:T(8,128)(2,1)S(1)}, u32[]{:S(2)}, u32[]{:S(2)}) %collective-permute-start.30) | collective-permute-done | bytes 1179680 | tf_op jit(solution)/shard_map/ppermute | solution.py:12
  280.7 12.9 %collective-permute-done.35 = bf16[2,128,1152]{2,1,0:T(8,128)(2,1)S(1)} collective-permute-done((bf16[2,128,1152]{2,1,0:T(8,128)(2,1)S(1)}, bf16[2,128,1152]{2,1,0:T(8,128)(2,1)S(1)}, u32[]{:S(2)}, u32[]{:S(2)}) %collective-permute-start.35) | collective-permute-done | bytes 589856 | tf_op jit(solution)/shard_map/ppermute | solution.py:12
  295.4 9.3 %collective-permute-done.31 = bf16[2,128,1152]{2,1,0:T(8,128)(2,1)S(1)} collective-permute-done((bf16[2,128,1152]{2,1,0:T(8,128)(2,1)S(1)}, bf16[2,128,1152]{2,1,0:T(8,128)(2,1)S(1)}, u32[]{:S(2)}, u32[]{:S(2)}) %collective-permute-start.31) | collective-permute-done | bytes 589856 | tf_op jit(solution)/shard_map/ppermute | solution.py:12
  307.4 12.0 %collective-permute-done.40 = bf16[1,128,1152]{2,1,0:T(8,128)(2,1)S(1)} collective-permute-done((bf16[1,128,1152]{2,1,0:T(8,128)(2,1)S(1)}, bf16[1,128,1152]{2,1,0:T(8,128)(2,1)S(1)}, u32[]{:S(2)}, u32[]{:S(2)}) %collective-permute-start.40) | collective-permute-done | bytes 294944 | tf_op jit(solution)/shard_map/ppermute | solution.py:12
  320.5 14.0 %collective-permute-done.36 = bf16[1,128,1152]{2,1,0:T(8,128)(2,1)S(1)} collective-permute-done((bf16[1,128,1152]{2,1,0:T(8,128)(2,1)S(1)}, bf16[1,128,1152]{2,1,0:T(8,128)(2,1)S(1)}, u32[]{:S(2)}, u32[]{:S(2)}) %collective-permute-start.36) | collective-permute-done | bytes 294944 | tf_op jit(solution)/shard_map/ppermute | solution.py:12
  337.0 11.6 %collective-permute-done.32 = bf16[1,128,1152]{2,1,0:T(8,128)(2,1)S(1)} collective-permute-done((bf16[1,128,1152]{2,1,0:T(8,128)(2,1)S(1)}, bf16[1,128,1152]{2,1,0:T(8,128)(2,1)S(1)}, u32[]{:S(2)}, u32[]{:S(2)}) %collective-permute-start.32) | collective-permute-done | bytes 294944 | tf_op jit(solution)/shard_map/ppermute | solution.py:12
  366.3 4.6 multiply_reduce_fusion.6
  390.0 40.0 %collective-permute-done.25 = bf16[8,128,1024]{2,1,0:T(8,128)(2,1)S(1)} collective-permute-done((bf16[8,128,1024]{2,1,0:T(8,128)(2,1)S(1)}, bf16[8,128,1024]{2,1,0:T(8,128)(2,1)S(1)}, u32[]{:S(2)}, u32[]{:S(2)}) %collective-permute-start.25) | collective-permute-done | bytes 2097184 | tf_op jit(solution)/shard_map/ppermute | solution.py:24
  435.2 21.7 %collective-permute-done.26 = bf16[4,128,1024]{2,1,0:T(8,128)(2,1)S(1)} collective-permute-done((bf16[4,128,1024]{2,1,0:T(8,128)(2,1)S(1)}, bf16[4,128,1024]{2,1,0:T(8,128)(2,1)S(1)}, u32[]{:S(2)}, u32[]{:S(2)}) %collective-permute-start.26) | collective-permute-done | bytes 1048608 | tf_op jit(solution)/shard_map/ppermute | solution.py:12
  459.3 11.3 %collective-permute-done.27 = bf16[2,128,1024]{2,1,0:T(8,128)(2,1)S(1)} collective-permute-done((bf16[2,128,1024]{2,1,0:T(8,128)(2,1)S(1)}, bf16[2,128,1024]{2,1,0:T(8,128)(2,1)S(1)}, u32[]{:S(2)}, u32[]{:S(2)}) %collective-permute-start.27) | collective-permute-done | bytes 524320 | tf_op jit(solution)/shard_map/ppermute | solution.py:12
  471.4 40.1 %psum.7 = f32[5,1024]{1,0:T(8,128)S(1)} all-reduce(f32[5,1024]{1,0:T(8,128)S(1)} %pad_maximum_fusion.23), channel_id=1, replica_groups=mesh['seq'=16,'wshard'=2] {'seq','wshard'}, use_global_device_ids=true, to_apply=%region_10.11 | all-reduce | flops 5120 | bytes 40960 | tf_op jit(solution)/shard_map/psum | solution.py:352
  (350 shorter events, 169.4 us)
Async XLA Ops:
  5.7 41.8 %collective-permute-start.5 = (bf16[4,2,1152]{2,0,1:T(4,128)(2,1)S(1)}, bf16[4,2,1152]{2,0,1:T(4,128)(2,1)S(1)}, u32[]{:S(2)}, u32[]{:S(2)}) collective-permute-start(bf16[4,2,1152]{2,0,1:T(4,128)(2,1)S(1)} %get-tuple-element.69), channel_id=1, source_target_pairs={{4,0},{8,4},{12,8},{16,12},{20,16},{24,20},{28,24},{5,1},{9,5},{13... | collective-permute-start | bytes 55304 | tf_op jit(solution)/shard_map/ppermute | solution.py:12
  7.0 41.0 %collective-permute-start.6 = (bf16[4,2,1152]{2,0,1:T(4,128)(2,1)S(1)}, bf16[4,2,1152]{2,0,1:T(4,128)(2,1)S(1)}, u32[]{:S(2)}, u32[]{:S(2)}) collective-permute-start(bf16[4,2,1152]{2,0,1:T(4,128)(2,1)S(1)} %get-tuple-element.69), channel_id=1, source_target_pairs={{4,2},{8,6},{12,10},{16,14},{20,18},{24,22},{28,26},{5,3},{9,7},{1... | collective-permute-start | bytes 55304 | tf_op jit(solution)/shard_map/ppermute | solution.py:12
  9.0 42.0 %collective-permute-start.2 = (bf16[3,1024,256]{2,1,0:T(8,128)(2,1)}, bf16[3,1024,256]{2,1,0:T(8,128)(2,1)}, u32[]{:S(2)}, u32[]{:S(2)}) collective-permute-start(bf16[3,1024,256]{2,1,0:T(8,128)(2,1)} %dynamic-slice_bitcast_fusion), channel_id=1, source_target_pairs={{0,1},{1,0},{2,3},{3,2},{4,5},{5,4},{6,7},{7,6},{8,9},{9,8},{10,11... | collective-permute-start | bytes 4718600 | tf_op jit(solution)/shard_map/ppermute | solution.py:24
  11.9 37.5 %collective-permute-start.3 = (bf16[4,2,1152]{2,0,1:T(4,128)(2,1)S(1)}, bf16[4,2,1152]{2,0,1:T(4,128)(2,1)S(1)}, u32[]{:S(2)}, u32[]{:S(2)}) collective-permute-start(bf16[4,2,1152]{2,0,1:T(4,128)(2,1)S(1)} %get-tuple-element.68), channel_id=1, source_target_pairs={{2,4},{6,8},{10,12},{14,16},{18,20},{22,24},{26,28},{3,5},{7,9},{1... | collective-permute-start | bytes 55304 | tf_op jit(solution)/shard_map/ppermute | solution.py:12
  77.2 29.5 %collective-permute-start.9 = (bf16[1024,1024]{1,0:T(8,128)(2,1)}, bf16[1024,1024]{1,0:T(8,128)(2,1)}, u32[]{:S(2)}, u32[]{:S(2)}) collective-permute-start(bf16[1024,1024]{1,0:T(8,128)(2,1)} %convolution_convert_fusion.4), channel_id=1, source_target_pairs={{0,2},{2,0},{4,6},{6,4},{8,10},{10,8},{12,14},{14,12},{16,18},{18,... | collective-permute-start | bytes 6291464 | tf_op jit(solution)/shard_map/ppermute | solution.py:12
  77.4 25.7 %collective-permute-start.17 = (bf16[512,1024]{1,0:T(8,128)(2,1)}, bf16[512,1024]{1,0:T(8,128)(2,1)}, u32[]{:S(2)}, u32[]{:S(2)}) collective-permute-start(bf16[512,1024]{1,0:T(8,128)(2,1)} %bitcast.18), channel_id=1, source_target_pairs={{0,1},{1,0},{2,3},{3,2},{4,5},{5,4},{6,7},{7,6},{8,9},{9,8},{10,11... | collective-permute-start | bytes 3145736 | tf_op jit(solution)/shard_map/ppermute | solution.py:24
  78.9 43.6 %collective-permute-start.15 = (bf16[512,1024]{1,0:T(8,128)(2,1)}, bf16[512,1024]{1,0:T(8,128)(2,1)}, u32[]{:S(2)}, u32[]{:S(2)}) collective-permute-start(bf16[512,1024]{1,0:T(8,128)(2,1)} %bitcast.18), channel_id=1, source_target_pairs={{0,2},{2,0},{4,6},{6,4},{8,10},{10,8},{12,14},{14,12},{16,18},{18,... | collective-permute-start | bytes 3145736 | tf_op jit(solution)/shard_map/ppermute | solution.py:12
  103.1 55.5 %collective-permute-start.18 = (bf16[512,1024]{1,0:T(8,128)(2,1)}, bf16[512,1024]{1,0:T(8,128)(2,1)}, u32[]{:S(2)}, u32[]{:S(2)}) collective-permute-start(bf16[512,1024]{1,0:T(8,128)(2,1)} %collective-permute-done.17), channel_id=1, source_target_pairs={{0,2},{2,0},{4,6},{6,4},{8,10},{10,8},{12,14},{14,12},{16,18},{18,... | collective-permute-start | bytes 3145736 | tf_op jit(solution)/shard_map/ppermute | solution.py:12
  111.9 26.5 %collective-permute-start.11 = (bf16[512,1024]{1,0:T(8,128)(2,1)S(1)}, bf16[512,1024]{1,0:T(8,128)(2,1)S(1)}, u32[]{:S(2)}, u32[]{:S(2)}) collective-permute-start(bf16[512,1024]{1,0:T(8,128)(2,1)S(1)} %slice.503), channel_id=1, source_target_pairs={{0,1},{1,0},{2,3},{3,2},{4,5},{5,4},{6,7},{7,6},{8,9},{9,8},{10,11... | collective-permute-start | bytes 3145736 | tf_op jit(solution)/shard_map/ppermute | solution.py:24
  144.8 203.9 %collective-permute-start.16 = (bf16[512,1024]{1,0:T(8,128)(2,1)}, bf16[512,1024]{1,0:T(8,128)(2,1)S(1)}, u32[]{:S(2)}, u32[]{:S(2)}) collective-permute-start(bf16[512,1024]{1,0:T(8,128)(2,1)} %slice.507), channel_id=1, source_target_pairs={{0,2},{2,0},{4,6},{6,4},{8,10},{10,8},{12,14},{14,12},{16,18},{18,... | collective-permute-start | bytes 3145736 | tf_op jit(solution)/shard_map/ppermute | solution.py:12
  177.3 42.1 %collective-permute-start.13 = (bf16[512,1024]{1,0:T(8,128)(2,1)}, bf16[512,1024]{1,0:T(8,128)(2,1)}, u32[]{:S(2)}, u32[]{:S(2)}) collective-permute-start(bf16[512,1024]{1,0:T(8,128)(2,1)} %slice.505), channel_id=1, source_target_pairs={{0,2},{2,0},{4,6},{6,4},{8,10},{10,8},{12,14},{14,12},{16,18},{18,... | collective-permute-start | bytes 3145736 | tf_op jit(solution)/shard_map/ppermute | solution.py:12
  187.5 35.1 %collective-permute-start.19 = (bf16[512,1024]{1,0:T(8,128)(2,1)}, bf16[512,1024]{1,0:T(8,128)(2,1)}, u32[]{:S(2)}, u32[]{:S(2)}) collective-permute-start(bf16[512,1024]{1,0:T(8,128)(2,1)} %slice.509), channel_id=1, source_target_pairs={{0,2},{2,0},{4,6},{6,4},{8,10},{10,8},{12,14},{14,12},{16,18},{18,... | collective-permute-start | bytes 3145736 | tf_op jit(solution)/shard_map/ppermute | solution.py:12
  198.5 29.1 %collective-permute-start.38 = (bf16[4,128,1152]{2,1,0:T(8,128)(2,1)}, bf16[4,128,1152]{2,1,0:T(8,128)(2,1)}, u32[]{:S(2)}, u32[]{:S(2)}) collective-permute-start(bf16[4,128,1152]{2,1,0:T(8,128)(2,1)} %pad_maximum_fusion.16), channel_id=1, source_target_pairs={{0,4},{2,6},{4,0},{6,2},{8,12},{10,14},{12,8},{14,10},{16,20},{18,... | collective-permute-start | bytes 3538952 | tf_op jit(solution)/shard_map/ppermute | solution.py:12
  209.8 43.1 %collective-permute-start.34 = (bf16[4,128,1152]{2,1,0:T(8,128)(2,1)}, bf16[4,128,1152]{2,1,0:T(8,128)(2,1)}, u32[]{:S(2)}, u32[]{:S(2)}) collective-permute-start(bf16[4,128,1152]{2,1,0:T(8,128)(2,1)} %pad_maximum_fusion.15), channel_id=1, source_target_pairs={{0,4},{2,6},{4,0},{6,2},{8,12},{10,14},{12,8},{14,10},{16,20},{18,... | collective-permute-start | bytes 3538952 | tf_op jit(solution)/shard_map/ppermute | solution.py:12
  220.3 129.4 %collective-permute-start.10 = (bf16[512,1024]{1,0:T(8,128)(2,1)S(1)}, bf16[512,1024]{1,0:T(8,128)(2,1)S(1)}, u32[]{:S(2)}, u32[]{:S(2)}) collective-permute-start(bf16[512,1024]{1,0:T(8,128)(2,1)S(1)} %copy-done.22), channel_id=1, source_target_pairs={{0,2},{2,0},{4,6},{6,4},{8,10},{10,8},{12,14},{14,12},{16,18},{18,... | collective-permute-start | bytes 3145736 | tf_op jit(solution)/shard_map/ppermute | solution.py:12
  222.6 54.8 %collective-permute-start.30 = (bf16[4,128,1152]{2,1,0:T(8,128)(2,1)S(1)}, bf16[4,128,1152]{2,1,0:T(8,128)(2,1)S(1)}, u32[]{:S(2)}, u32[]{:S(2)}) collective-permute-start(bf16[4,128,1152]{2,1,0:T(8,128)(2,1)S(1)} %pad_maximum_fusion.14), channel_id=1, source_target_pairs={{0,4},{2,6},{4,0},{6,2},{8,12},{10,14},{12,8},{14,10},{16,20},{18,... | collective-permute-start | bytes 3538952 | tf_op jit(solution)/shard_map/ppermute | solution.py:12
  227.6 122.1 %collective-permute-start.14 = (bf16[512,1024]{1,0:T(8,128)(2,1)S(1)}, bf16[512,1024]{1,0:T(8,128)(2,1)S(1)}, u32[]{:S(2)}, u32[]{:S(2)}) collective-permute-start(bf16[512,1024]{1,0:T(8,128)(2,1)S(1)} %add_convert_fusion.5), channel_id=1, source_target_pairs={{0,1},{1,0},{2,3},{3,2},{4,5},{5,4},{6,7},{7,6},{8,9},{9,8},{10,11... | collective-permute-start | bytes 3145736 | tf_op jit(solution)/shard_map/ppermute | solution.py:24
  252.9 26.2 %collective-permute-start.39 = (bf16[2,128,1152]{2,1,0:T(8,128)(2,1)S(1)}, bf16[2,128,1152]{2,1,0:T(8,128)(2,1)S(1)}, u32[]{:S(2)}, u32[]{:S(2)}) collective-permute-start(bf16[2,128,1152]{2,1,0:T(8,128)(2,1)S(1)} %add_convert_fusion.6), channel_id=1, source_target_pairs={{0,8},{2,10},{4,12},{6,14},{8,0},{10,2},{12,4},{14,6},{16,24},{18,... | collective-permute-start | bytes 1769480 | tf_op jit(solution)/shard_map/ppermute | solution.py:12
  279.1 25.6 %collective-permute-start.31 = (bf16[2,128,1152]{2,1,0:T(8,128)(2,1)S(1)}, bf16[2,128,1152]{2,1,0:T(8,128)(2,1)S(1)}, u32[]{:S(2)}, u32[]{:S(2)}) collective-permute-start(bf16[2,128,1152]{2,1,0:T(8,128)(2,1)S(1)} %add_convert_fusion.8), channel_id=1, source_target_pairs={{0,8},{2,10},{4,12},{6,14},{8,0},{10,2},{12,4},{14,6},{16,24},{18,... | collective-permute-start | bytes 1769480 | tf_op jit(solution)/shard_map/ppermute | solution.py:12
  293.7 55.1 %collective-permute-start.20 = (bf16[512,1024]{1,0:T(8,128)(2,1)S(1)}, bf16[512,1024]{1,0:T(8,128)(2,1)S(1)}, u32[]{:S(2)}, u32[]{:S(2)}) collective-permute-start(bf16[512,1024]{1,0:T(8,128)(2,1)S(1)} %add_convert_fusion.3), channel_id=1, source_target_pairs={{0,1},{1,0},{2,3},{3,2},{4,5},{5,4},{6,7},{7,6},{8,9},{9,8},{10,11... | collective-permute-start | bytes 3145736 | tf_op jit(solution)/shard_map/ppermute | solution.py:24
  381.6 48.4 %collective-permute-start.25 = (bf16[8,128,1024]{2,1,0:T(8,128)(2,1)S(1)}, bf16[8,128,1024]{2,1,0:T(8,128)(2,1)S(1)}, u32[]{:S(2)}, u32[]{:S(2)}) collective-permute-start(bf16[8,128,1024]{2,1,0:T(8,128)(2,1)S(1)} %dynamic-slice_dynamic-update-slice_fusion), channel_id=1, source_target_pairs={{0,1},{1,0},{2,3},{3,2},{4,5},{5,4},{6,7},{7,6},{8,9},{9,8},{10,11... | collective-permute-start | bytes 6291464 | tf_op jit(solution)/shard_map/ppermute | solution.py:24
  388.7 45.7 %collective-permute-start.24 = (bf16[512,1024]{1,0:T(8,128)(2,1)S(1)}, bf16[512,1024]{1,0:T(8,128)(2,1)S(1)}, u32[]{:S(2)}, u32[]{:S(2)}) collective-permute-start(bf16[512,1024]{1,0:T(8,128)(2,1)S(1)} %slice.522), channel_id=1, source_target_pairs={{0,2},{2,0},{4,6},{6,4},{8,10},{10,8},{12,14},{14,12},{16,18},{18,... | collective-permute-start | bytes 3145736 | tf_op jit(solution)/shard_map/ppermute | solution.py:12
  430.4 26.4 %collective-permute-start.26 = (bf16[4,128,1024]{2,1,0:T(8,128)(2,1)S(1)}, bf16[4,128,1024]{2,1,0:T(8,128)(2,1)S(1)}, u32[]{:S(2)}, u32[]{:S(2)}) collective-permute-start(bf16[4,128,1024]{2,1,0:T(8,128)(2,1)S(1)} %add_convert_fusion.2), channel_id=1, source_target_pairs={{0,4},{2,6},{4,0},{6,2},{8,12},{10,14},{12,8},{14,10},{16,20},{18,... | collective-permute-start | bytes 3145736 | tf_op jit(solution)/shard_map/ppermute | solution.py:12
  471.4 41.4 %collective-permute-start.28 = (bf16[1,128,1024]{2,1,0:T(8,128)(2,1)S(1)}, bf16[1,128,1024]{2,1,0:T(8,128)(2,1)S(1)}, u32[]{:S(2)}, u32[]{:S(2)}) collective-permute-start(bf16[1,128,1024]{2,1,0:T(8,128)(2,1)S(1)} %add_convert_fusion.13), channel_id=1, source_target_pairs={{0,16},{2,18},{4,20},{6,22},{8,24},{10,26},{12,28},{14,30},{16,0},... | collective-permute-start | bytes 786440 | tf_op jit(solution)/shard_map/ppermute | solution.py:12
  (73 other events, 797.5 us)

commit v2 on v0

v2 whole, which is shorter than its diff:
```python
import functools

import jax
import jax.numpy as jnp
from jax import lax
from jax.experimental import pallas as pl
from jax.experimental.pallas import tpu as pltpu
from jax.sharding import PartitionSpec as P

EPS = 1e-05
LOW = jnp.bfloat16
F32 = jnp.float32
TILE = 256
NT = (((1,), (1,)), ((), ()))
TN = (((0,), (0,)), ((), ()))


def over_seq(block, route):
    return lax.ppermute(block, "seq", route)


def swap_seq(block, mask):
    return over_seq(block, [(i, i ^ mask) for i in range(lax.axis_size("seq"))])


def swap_core(block):
    return swap_seq(block, 1)


def swap_pair(block):
    return lax.ppermute(block, "wshard", [(0, 1), (1, 0)])


def swap(block, link):
    return swap_pair(block) if link == "pair" else swap_seq(block, 2 * link)


def tie(value, *after):
    return lax.optimization_barrier((value,) + after)[0]


def dot(left, right):
    return jnp.dot(left, right, preferred_element_type=F32)


def dot_nt(left, right):
    return lax.dot_general(left, right, NT, preferred_element_type=F32)


def dot_tn(left, right):
    return lax.dot_general(left, right, TN, preferred_element_type=F32)


def call(body, name, grid, in_specs, out_specs, out_shape, scratch=(), scalars=1, aliases=None):
    return pl.pallas_call(
        body,
        grid_spec=pltpu.PrefetchScalarGridSpec(
            num_scalar_prefetch=scalars,
            grid=grid,
            in_specs=in_specs,
            out_specs=out_specs,
            scratch_shapes=list(scratch),
        ),
        out_shape=out_shape,
        input_output_aliases=aliases or {},
        compiler_params=pltpu.CompilerParams(vmem_limit_bytes=56 * 2**20),
        cost_estimate=pl.CostEstimate(flops=1000, bytes_accessed=1000, transcendentals=0),
        name=name,
    )


def shape(rows, cols, kind=LOW):
    return jax.ShapeDtypeStruct((rows, cols), kind)


def whole(array):
    zeros = (0,) * array.ndim
    return pl.BlockSpec(array.shape, lambda *_: zeros)


def normed(values, gain):
    wide = values.astype(F32)
    scale = lax.rsqrt(jnp.mean(wide * wide, axis=-1, keepdims=True) + EPS)
    return wide * scale * gain, scale


def piece_columns(place, j, depth):
    return pl.ds(pl.multiple_of((place ^ j) * depth, depth), depth)


def conv_forward_body(
    block,
    idx,
    x_ref,
    edge_ref,
    in_ref,
    out_ref,
    r0,
    r1,
    r2,
    r3,
    gain_ref,
    taps_ref,
    keep_ref,
    normed_ref,
    parts_ref,
    conv_in_ref,
    conv_out_ref,
    mixed_ref,
    mix_ref,
    c_edge_ref,
    nx,
    edge_in,
    acc,
):
    step = pl.program_id(0)
    place = idx[1]
    far = (r0, r1, r2, r3)
    depth = r0.shape[1]
    half = r0.shape[2]
    cols = 2 * half
    gain = gain_ref[...]

    def project(load, j):
        mine = dot(load(slice(None)), in_ref[j])
        other = None
        for p in range(4):
            term = dot(load(piece_columns(place, p, depth)), far[p][j])
            other = term if other is None else other + term
        return jnp.concatenate([mine, other], axis=1)

    @pl.when(step == 0)
    def _():
        count = edge_ref.shape[0]
        nx[:count] = normed(edge_ref[...], gain)[0].astype(LOW)

        def load(columns):
            return nx[:count, columns]

        before = count // 2
        edge_b, edge_c, edge_x = (project(load, j) for j in range(3))
        edge_in[...] = (edge_b[:before] * edge_x[:before]).astype(LOW).astype(F32)
        c_edge_ref[...] = edge_c[before:]

    nx[...] = normed(x_ref[...], gain)[0].astype(LOW)
    normed_ref[...] = nx[...]

    def load(columns):
        return nx[:, columns]

    b_part, c_part, x_part = (project(load, j) for j in range(3))
    parts_ref[:, :cols] = b_part.astype(LOW)
    parts_ref[:, cols : 2 * cols] = c_part.astype(LOW)
    parts_ref[:, 2 * cols :] = x_part.astype(LOW)
    low_in = (b_part * x_part).astype(LOW)
    conv_in_ref[...] = low_in
    conv_in = low_in.astype(F32)
    groups = x_ref.shape[0] // block
    row = lax.broadcasted_iota(jnp.int32, (block, cols), 0)
    for g in range(groups):
        span = slice(g * block, (g + 1) * block)
        here = conv_in[span]
        base = step * 2 * groups + 2 * g
        two_before = edge_in[pl.ds(base, 1), :]
        one_before = edge_in[pl.ds(base + 1, 1), :]
        lag_one = jnp.where(row == 0, one_before, pltpu.roll(here, 1, 0))
        lag_two = jnp.where(
            row == 0, two_before, jnp.where(row == 1, one_before, pltpu.roll(here, 2, 0))
        )
        conv_out = (
            taps_ref[2:3, :] * here
            + taps_ref[1:2, :] * (keep_ref[span, 0:1] * lag_one)
            + taps_ref[0:1, :] * (keep_ref[span, 1:2] * lag_two)
        )
        conv_out_ref[span, :] = conv_out.astype(LOW)
        mixed_ref[span, :] = (c_part[span] * conv_out).astype(LOW)
    mixed = mixed_ref[...]
    acc[...] = dot(mixed[:, :half], out_ref[...])
    for p in range(4):
        where = piece_columns(place, p, depth)
        acc[:, where] += dot(mixed[:, half:], far[p][3])
    mix_ref[...] = acc[...].astype(LOW)


def conv_forward(idx, x, edges, in_weight, out_weight, far, gain, taps, keeps, block):
    total, width = x.shape
    rows = TILE
    half = far[0].shape[2]
    cols = 2 * half

    def rowed(columns):
        return pl.BlockSpec((rows, columns), lambda i, s: (i, 0))

    before = edges.shape[0] // 2
    return call(
        functools.partial(conv_forward_body, block),
        "conv_forward",
        (total // rows,),
        [
            rowed(width),
            whole(edges),
            pl.BlockSpec((3, width, half), lambda i, s: (0, 0, s[0])),
            pl.BlockSpec((half, width), lambda i, s: (s[0], 0)),
            *[whole(piece) for piece in far],
            whole(gain),
            whole(taps),
            rowed(keeps.shape[1]),
        ],
        [
            rowed(width),
            rowed(3 * cols),
            rowed(cols),
            rowed(cols),
            rowed(cols),
            rowed(width),
            pl.BlockSpec((before, cols), lambda i, s: (0, 0)),
        ],
        [
            shape(total, width),
            shape(total, 3 * cols),
            shape(total, cols),
            shape(total, cols),
            shape(total, cols),
            shape(total, width),
            shape(before, cols, F32),
        ],
        [
            pltpu.VMEM((rows, width), LOW),
            pltpu.VMEM((before, cols), F32),
            pltpu.VMEM((rows, width), F32),
        ],
    )(idx, x, edges, in_weight, out_weight, *far, gain, taps, keeps)


def second_norm_body(x_ref, mine_ref, came_ref, gain_ref, low_ref, *resid_ref):
    two = x_ref[...].astype(F32) + (mine_ref[...].astype(F32) + came_ref[...].astype(F32))
    low_ref[...] = normed(two, gain_ref[...])[0].astype(LOW)
    for ref in resid_ref:
        ref[...] = two


def second_norm(x, mine, came, gain, which, keep):
    rows, width = x.shape[0] // 2, x.shape[1]
    tile = rows // 4

    def plain(start):
        return pl.BlockSpec((tile, width), lambda i: (i + 4 * start, 0))

    return call(
        second_norm_body,
        "second_norm",
        (4,),
        [plain(which), plain(which), plain(1 - which), whole(gain)],
        [plain(0)] * (1 + keep),
        [shape(rows, width), shape(rows, width, F32)][: 1 + keep],
        scalars=0,
    )(x, mine, came, gain)


def feed_forward_body(count, held, idx, *refs):
    x_refs, ct_refs = refs[:2], refs[2:4]
    gate_hbm, up_hbm, down_hbm = refs[4:7]
    refs = refs[7 + held :]
    act_ref, d_gate_ref, d_up_ref, term_a, term_b, d_a, d_b, gate_ref, up_ref, down_ref, sems = refs
    step = pl.program_id(0)
    first = step < count
    units = gate_ref.shape[1]
    mine = pl.ds(pl.multiple_of(idx[0] * units, 128), units)
    copies = [
        pltpu.make_async_copy(gate_hbm.at[:, mine], gate_ref, sems.at[0]),
        pltpu.make_async_copy(up_hbm.at[:, mine], up_ref, sems.at[1]),
        pltpu.make_async_copy(down_hbm.at[mine, :], down_ref, sems.at[2]),
    ]

    def there(copy):
        @pl.when(step == 0)
        def _():
            copy.wait()

    @pl.when(step == 0)
    def _():
        for copy in copies:
            copy.start()

    x = jnp.where(first, x_refs[0][...], x_refs[1][...])
    upstream = jnp.where(first, ct_refs[0][...], ct_refs[1][...])
    there(copies[0])
    gate = dot(x, gate_ref[...])
    there(copies[1])
    up_value = dot(x, up_ref[...])
    there(copies[2])
    d_act = dot_nt(upstream, down_ref[...])
    sigma = jax.nn.sigmoid(gate)
    silu_gate = gate * sigma
    act = (silu_gate * up_value).astype(LOW)
    d_gate = (d_act * up_value * (sigma * (1.0 + gate * (1.0 - sigma)))).astype(LOW)
    d_up = (d_act * silu_gate).astype(LOW)
    act_ref[...] = act
    d_gate_ref[...] = d_gate
    d_up_ref[...] = d_up
    d_normed = (dot_nt(d_gate, gate_ref[...]) + dot_nt(d_up, up_ref[...])).astype(LOW)
    term = dot(act, down_ref[...]).astype(LOW)

    @pl.when(first)
    def _():
        d_a[...] = d_normed
        term_a[...] = term

    @pl.when(step >= count)
    def _():
        d_b[...] = d_normed
        term_b[...] = term


def feed_forward(idx, xs, cts, weights, total, start, held):
    gate, up, down = weights
    rows, width = xs[0].shape
    units = gate.shape[1] // 2
    count = rows // TILE

    def rowed(index):
        return pl.BlockSpec((TILE, width), index)

    def lower(i, s):
        return (jnp.minimum(i, count - 1), 0)

    def upper(i, s):
        return (jnp.maximum(i - count, 0), 0)

    any_spec = pl.BlockSpec(memory_space=pl.ANY)
    unit_spec = pl.BlockSpec((TILE, units), lambda i, s: (i + start, 0))
    return call(
        functools.partial(feed_forward_body, count, len(held)),
        "feed_forward",
        (2 * count,),
        [rowed(lower), rowed(upper)] * 2 + [any_spec] * (3 + len(held)),
        [unit_spec] * 3 + [rowed(lower), rowed(upper)] * 2,
        [shape(total, units)] * 3 + [shape(rows, width)] * 4,
        [
            pltpu.VMEM((width, units), LOW),
            pltpu.VMEM((width, units), LOW),
            pltpu.VMEM((units, width), LOW),
            pltpu.SemaphoreType.DMA((3,)),
        ],
        aliases={8 + k: k for k in range(len(held))},
    )(idx, *xs, *cts, gate, up, down, *held)


def slot_masks(order):
    masks = [0]
    for link in reversed(order):
        masks = masks + [mask ^ link for mask in masks]
    return masks


def grads_body(pieces, count, chips, slots, *refs):
    x_hbm, refs = refs[:pieces], refs[pieces:]
    y_hbm, refs = refs[:count], refs[count:]
    outs, refs = refs[: 2 * count], refs[2 * count :]
    x_buf, y_buf, acc, out_buf, x_sems, y_sems, out_sems = refs
    depth = x_buf.shape[1]

    def x_copy(k):
        return pltpu.make_async_copy(x_hbm[k], x_buf.at[k], x_sems.at[k])

    def y_copy(a, k):
        rows = pl.ds(k * depth, depth)
        return pltpu.make_async_copy(y_hbm[a].at[rows], y_buf.at[a, k], y_sems.at[a, k])

    for k in range(pieces):
        x_copy(k).start()
        y_copy(0, k).start()
    for a in range(1, count):
        for k in range(pieces):
            y_copy(a, k).start()
    rows = acc.shape[0] // chips
    send_first = chips // 2
    out_copies = []
    for a in range(count):
        for k in range(pieces):
            if a == 0:
                x_copy(k).wait()
            y_copy(a, k).wait()
            term = dot_tn(x_buf[k], y_buf[a, k])
            if k == 0:
                acc[...] = term
            else:
                acc[...] += term
        for slot in range(chips):
            where = pl.ds(pl.multiple_of(slots[a * chips + slot] * rows, rows), rows)
            out_buf[a, slot] = acc[where, :].astype(LOW)
        sent = pltpu.make_async_copy(out_buf.at[a, pl.ds(send_first, chips // 2)], outs[2 * a], out_sems.at[a, 0])
        kept = pltpu.make_async_copy(out_buf.at[a, pl.ds(0, send_first)], outs[2 * a + 1], out_sems.at[a, 1])
        sent.start()
        kept.start()
        out_copies += [sent, kept]
    for copy in out_copies:
        copy.wait()


def weight_grads(slots, chips, xs, ys):
    depth, width = xs[0].shape
    units = ys[0].shape[1]
    pieces, count = len(xs), len(ys)
    any_spec = pl.BlockSpec(memory_space=pl.ANY)
    out = jax.ShapeDtypeStruct((chips // 2, width // chips, units), LOW)
    return call(
        functools.partial(grads_body, pieces, count, chips),
        "weight_grads",
        (),
        [any_spec] * (pieces + count),
        [any_spec] * (2 * count),
        [out] * (2 * count),
        [
            pltpu.VMEM((pieces, depth, width), LOW),
            pltpu.VMEM((count, pieces, depth, units), LOW),
            pltpu.VMEM((width, units), F32),
            pltpu.VMEM((count, chips, width // chips, units), LOW),
            pltpu.SemaphoreType.DMA((pieces,)),
            pltpu.SemaphoreType.DMA((count, pieces)),
            pltpu.SemaphoreType.DMA((count, 2)),
        ],
    )(slots, *xs, *ys)


def norm_back(upstream, values, scale, gain):
    scaled = values * scale
    weighted = upstream * gain
    inner = jnp.mean(weighted * scaled, axis=-1, keepdims=True)
    return scale * (weighted - scaled * inner), upstream * scaled


def resid_back_body(mine_ref, near_ref, far_ref, two_ref, cot_ref, gain_ref, d_ref, low_ref, sum_ref):
    step = pl.program_id(0)
    upstream = mine_ref[...].astype(F32) + near_ref[...].astype(F32) + far_ref[...].astype(F32)
    two = two_ref[...]
    scale = lax.rsqrt(jnp.mean(two * two, axis=-1, keepdims=True) + EPS)
    back, terms = norm_back(upstream, two, scale, gain_ref[...])
    d_resid = cot_ref[...].astype(F32) + back
    d_ref[...] = d_resid
    low_ref[...] = d_resid.astype(LOW)
    part = jnp.sum(terms.reshape(-1, 8, terms.shape[1]), axis=0)

    @pl.when(step == 0)
    def _():
        sum_ref[...] = part

    @pl.when(step > 0)
    def _():
        sum_ref[...] += part


def resid_back(mine, near, far, two, cot, gain):
    rows, width = two.shape

    def plain(kind=None):
        return pl.BlockSpec((TILE, width), lambda i: (i, 0))

    return call(
        resid_back_body,
        "resid_back",
        (rows // TILE,),
        [plain()] * 5 + [whole(gain)],
        [plain(), plain(), pl.BlockSpec((8, width), lambda i: (0, 0))],
        [shape(rows, width, F32), shape(rows, width), shape(8, width, F32)],
        scalars=0,
    )(mine, near, far, two, cot, gain)


def conv_back_body(
    block,
    count,
    chips,
    idx,
    slots,
    own_ref,
    other_ref,
    edge_ref,
    normed_ref,
    mixed_ref,
    parts_ref,
    conv_in_ref,
    conv_out_ref,
    c_edge_ref,
    in_ref,
    out_ref,
    r0,
    r1,
    r2,
    r3,
    taps_ref,
    keep_ref,
    own_normed_ref,
    other_normed_ref,
    taps_out_ref,
    send_a,
    keep_a,
    send_b,
    keep_b,
    held,
    edge_d,
    acc,
    d_proj,
    in_acc,
    out_acc,
    bufs,
    sems,
):
    step = pl.program_id(0)
    place = idx[1]
    far = (r0, r1, r2, r3)
    depth = r0.shape[1]
    half = r0.shape[2]
    cols = 2 * half

    def back_out(load):
        mine = dot_nt(load(slice(None)), out_ref[...])
        other = None
        for p in range(4):
            term = dot_nt(load(piece_columns(place, p, depth)), far[p][3])
            other = term if other is None else other + term
        return jnp.concatenate([mine, other], axis=1)

    @pl.when(step == 0)
    def _():
        edge_d[...] = back_out(lambda columns: edge_ref[:, columns]) * c_edge_ref[...]
        in_acc[...] = jnp.zeros_like(in_acc)
        out_acc[...] = jnp.zeros_like(out_acc)
        taps_out_ref[...] = jnp.zeros_like(taps_out_ref)

    held[...] = jnp.where(step < count, own_ref[...], other_ref[...])
    d_mixed = back_out(lambda columns: held[:, columns])
    d_conv = d_mixed * parts_ref[:, cols : 2 * cols].astype(F32)
    d_proj[:, cols : 2 * cols] = (d_mixed * conv_out_ref[...].astype(F32)).astype(LOW)
    groups = own_ref.shape[0] // block
    row = lax.broadcasted_iota(jnp.int32, (block, cols), 0)
    for g in range(groups):
        span = slice(g * block, (g + 1) * block)
        here = d_conv[span]
        base = step * 2 * groups + 2 * g
        after_one = edge_d[pl.ds(base, 1), :]
        after_two = edge_d[pl.ds(base + 1, 1), :]
        next_one = jnp.where(row == block - 1, after_one, pltpu.roll(here, block - 1, 0))
        next_two = jnp.where(
            row == block - 1,
            after_two,
            jnp.where(row == block - 2, after_one, pltpu.roll(here, block - 2, 0)),
        )
        next_one = keep_ref[span, 2:3] * next_one
        next_two = keep_ref[span, 3:4] * next_two
        d_in = taps_ref[2:3, :] * here + taps_ref[1:2, :] * next_one + taps_ref[0:1, :] * next_two
        conv_in = conv_in_ref[span, :].astype(F32)
        for k, term in enumerate((next_two, next_one, here)):
            taps_out_ref[k] += jnp.sum((term * conv_in).reshape(-1, 8, cols), axis=0)
        d_proj[span, :cols] = (d_in * parts_ref[span, 2 * cols :].astype(F32)).astype(LOW)
        d_proj[span, 2 * cols :] = (d_in * parts_ref[span, :cols].astype(F32)).astype(LOW)
    out_acc[...] += dot_tn(held[...], mixed_ref[...])
    in_acc[...] += dot_tn(normed_ref[...], d_proj[...])
    total = None
    for j in range(3):
        term = dot_nt(d_proj[:, j * cols : j * cols + half], in_ref[j])
        total = term if total is None else total + term
    acc[...] = total
    for p in range(4):
        where = piece_columns(place, p, depth)
        total = None
        for j in range(3):
            term = dot_nt(d_proj[:, j * cols + half : (j + 1) * cols], far[p][j])
            total = term if total is None else total + term
        acc[:, where] += total

    @pl.when(step < count)
    def _():
        own_normed_ref[...] = acc[...].astype(LOW)

    @pl.when(step >= count)
    def _():
        other_normed_ref[...] = acc[...].astype(LOW)

    @pl.when(step == 2 * count - 1)
    def _():
        rows = in_acc.shape[0] // chips
        copies = []
        for a, (halves, keeps, sends) in enumerate(
            (
                (((out_acc, 0), (in_acc, 0)), keep_a, send_a),
                (((in_acc, cols), (in_acc, 2 * cols)), keep_b, send_b),
            )
        ):
            for slot in range(2 * chips):
                number = a * 2 * chips + slot
                where = pl.ds(pl.multiple_of(slots[number] * rows, rows), rows)
                other = slot_pair(a, slot, chips)
                for at, (source, start) in enumerate(halves):
                    low = start + other * half
                    bufs[a, slot, :, at * half : (at + 1) * half] = source[
                        where, low : low + half
                    ].astype(LOW)
            sent = pltpu.make_async_copy(bufs.at[a, pl.ds(chips, chips)], sends, sems.at[a, 0])
            kept = pltpu.make_async_copy(bufs.at[a, pl.ds(0, chips)], keeps, sems.at[a, 1])
            sent.start()
            kept.start()
            copies += [sent, kept]
        for copy in copies:
            copy.wait()


def slot_pair(group, slot, chips):
    return slot // chips if group == 0 else (slot // (chips // 2)) % 2


def mix_orders(links):
    return ["pair"] + links, [links[0], "pair"] + links[1:]


def conv_back(idx, slots, chips, own, other, edges, kept, in_weight, out_weight, far, taps, keeps, block):
    normed_mix, parts, conv_in, conv_out, mixed, c_edge = kept
    rows, width = own.shape
    half = far[0].shape[2]
    cols = 2 * half
    tile = TILE
    count = rows // tile

    def rowed(columns):
        return pl.BlockSpec((tile, columns), lambda i, s, t: (i, 0))

    def fixed(array):
        zeros = (0,) * array.ndim
        return pl.BlockSpec(array.shape, lambda i, s, t: zeros)

    lower = pl.BlockSpec((tile, width), lambda i, s, t: (jnp.minimum(i, count - 1), 0))
    upper = pl.BlockSpec((tile, width), lambda i, s, t: (jnp.maximum(i - count, 0), 0))
    any_spec = pl.BlockSpec(memory_space=pl.ANY)
    grad = jax.ShapeDtypeStruct((chips, width // chips, cols), LOW)
    return call(
        functools.partial(conv_back_body, block, count, chips),
        "conv_back",
        (2 * count,),
        [
            lower,
            upper,
            fixed(edges),
            rowed(width),
            rowed(cols),
            rowed(3 * cols),
            rowed(cols),
            rowed(cols),
            fixed(c_edge),
            pl.BlockSpec((3, width, half), lambda i, s, t: (0, 0, s[0])),
            pl.BlockSpec((half, width), lambda i, s, t: (s[0], 0)),
            *[fixed(piece) for piece in far],
            fixed(taps),
            rowed(keeps.shape[1]),
        ],
        [lower, upper, pl.BlockSpec((3, 8, cols), lambda i, s, t: (0, 0, 0))] + [any_spec] * 4,
        [
            shape(rows, width),
            shape(rows, width),
            jax.ShapeDtypeStruct((3, 8, cols), F32),
        ]
        + [grad] * 4,
        [
            pltpu.VMEM((tile, width), LOW),
            pltpu.VMEM((edges.shape[0], cols), F32),
            pltpu.VMEM((tile, width), F32),
            pltpu.VMEM((tile, 3 * cols), LOW),
            pltpu.VMEM((width, 3 * cols), F32),
            pltpu.VMEM((width, cols), F32),
            pltpu.VMEM((2, 2 * chips, width // chips, cols), LOW),
            pltpu.SemaphoreType.DMA((2, 2)),
        ],
        scalars=2,
    )(
        idx,
        slots,
        own,
        other,
        edges,
        normed_mix,
        mixed,
        parts,
        conv_in,
        conv_out,
        c_edge,
        in_weight,
        out_weight,
        *far,
        taps,
        keeps,
    )


def hidden_back_body(mine_ref, came_ref, x_ref, d_ref, gain_ref, out_ref, sum_ref):
    step = pl.program_id(0)
    upstream = mine_ref[...].astype(F32) + came_ref[...].astype(F32)
    resid = x_ref[...].astype(F32)
    scale = lax.rsqrt(jnp.mean(resid * resid, axis=-1, keepdims=True) + EPS)
    back, terms = norm_back(upstream, resid, scale, gain_ref[...])
    out_ref[...] = d_ref[...] + back
    part = jnp.sum(terms.reshape(-1, 8, terms.shape[1]), axis=0)

    @pl.when(step == 0)
    def _():
        sum_ref[...] = part

    @pl.when(step > 0)
    def _():
        sum_ref[...] += part


def hidden_back(mine, came, x, d_resid, gain):
    rows, width = x.shape
    plain = pl.BlockSpec((TILE, width), lambda i: (i, 0))
    return call(
        hidden_back_body,
        "hidden_back",
        (rows // TILE,),
        [plain] * 4 + [whole(gain)],
        [plain, pl.BlockSpec((8, width), lambda i: (0, 0))],
        [shape(rows, width, F32), shape(8, width, F32)],
        scalars=0,
    )(mine, came, x, d_resid, gain)


class Halving:
    def __init__(self, keep, order):
        self.terms = [keep]
        self.half = keep.shape[0]
        self.links = list(order)

    def start(self, send):
        self.terms.append(swap(send, self.links.pop(0)))

    def step(self, *after):
        self.half //= 2
        half = self.half
        terms = self.terms
        if after:
            terms = [tie(terms[0], *after)] + terms[1:]
        going = sum(term[half : 2 * half].astype(F32) for term in terms).astype(LOW)
        self.terms.append(swap(going, self.links.pop(0)))

    def done(self):
        return sum(term[0].astype(F32) for term in self.terms)


def local(
    hidden,
    segments,
    cotangent,
    in_weight,
    out_weight,
    gate_weight,
    up_weight,
    down_weight,
    conv_weight,
    norm_mix,
    norm_ffn,
):
    groups, block, width = hidden.shape
    rows = groups * block
    size = lax.axis_size("seq")
    seq_index = lax.axis_index("seq")
    core = seq_index % 2
    chip = seq_index // 2
    pair = lax.axis_index("wshard")
    first_core = core == 0
    chips = size // 2
    links = [1 << bit for bit in range(chips.bit_length() - 1)]
    turned = [links[1], links[0]] + links[2:]
    half = out_weight.shape[0] // 2
    cols = 2 * half
    place = chip & 3
    idx = jnp.stack([core, place]).astype(jnp.int32)

    def slots_of(*orders):
        masks = [mask for order in orders for mask in slot_masks(order)]
        return (chip ^ jnp.array(masks, jnp.int32)).astype(jnp.int32)

    weights = (gate_weight, up_weight, down_weight)

    def ordered(flag, mine, other, axis):
        return jnp.where(
            flag,
            jnp.concatenate([mine, other], axis=axis),
            jnp.concatenate([other, mine], axis=axis),
        )

    small = jnp.concatenate([conv_weight, norm_mix[None], norm_ffn[None]], axis=0)
    in_planes = jnp.transpose(in_weight, (1, 0, 2))
    depth = width // 4

    def piece(number):
        from_in = lax.dynamic_slice(in_planes, (0, number * depth, core * half), (3, depth, half))
        from_out = lax.dynamic_slice(out_weight, (core * half, number * depth), (half, depth))
        return jnp.concatenate([from_in, from_out[None]], axis=0)

    sent_zero = piece(place)
    sent_three = piece(place ^ 3)
    piece_zero = swap_pair(sent_zero)
    piece_three = swap_pair(sent_three)
    small_other = swap_pair(tie(small, sent_zero))
    piece_one = swap(piece_zero, 1)
    piece_two = swap(piece_zero, 2)
    far_weights = (piece_zero, piece_one, piece_two, piece_three)

    hidden, segments = lax.optimization_barrier((hidden, segments, sent_zero, sent_three))[:2]
    own = hidden.reshape(rows, width)
    other = swap_core(own)
    chip_hidden = jnp.concatenate([own, other], axis=0)
    cot = cotangent.reshape(rows, width)
    cot_far = swap_pair(tie(cot, piece_zero))

    seg_low = segments.astype(LOW)
    seg_other = swap_core(seg_low)

    def with_seg(values, segs):
        return jnp.concatenate(
            [values, jnp.broadcast_to(segs[:, :, None], (groups, segs.shape[1], 128))], axis=2
        )

    def ends(values, segs):
        both = values.reshape(groups, block, width)
        return (
            with_seg(both[:, :2], segs[:, :2]),
            with_seg(both[:, block - 2 :], segs[:, block - 2 :]),
        )

    head, last = ends(own, seg_low)
    other_head, other_last = ends(other, seg_other)
    even = range(2, size, 2)
    forth = [(i - 2, i) for i in range(2, size)]
    back = [(i, i - 2) for i in range(2, size)]
    from_before = over_seq(jnp.where(first_core, other_last, last), forth)
    from_after = over_seq(jnp.where(first_core, head, other_head), back)

    def after_blocks(outside, own_head, near_head):
        return jnp.where(
            first_core, jnp.stack([near_head, outside]), jnp.stack([outside, own_head])
        )

    before = jnp.where(
        first_core, jnp.stack([from_before, last]), jnp.stack([other_last, from_before])
    )
    after = after_blocks(from_after, head, other_head)
    edges = jnp.concatenate([before, after], axis=0)
    edge_rows = edges[..., :width].reshape(8 * groups, width)
    edge_segs = edges[..., width]
    segs = jnp.stack([seg_low, seg_other])
    segs_ext = jnp.concatenate([edge_segs[:2], segs, edge_segs[2:]], axis=2)
    keeps = jnp.stack(
        [(segs_ext[:, :, at : at + block] == segs).astype(F32) for at in (1, 0, 3, 4)], axis=-1
    ).reshape(2 * rows, 4)

    gains = ordered(pair == 0, small[3:], small_other[3:], 1).astype(F32)
    gain_mix, gain_ffn = gains[:1], gains[1:]
    taps = jnp.concatenate(
        [lax.dynamic_slice_in_dim(part[:3], core * half, half, 1) for part in (small, small_other)],
        axis=1,
    ).astype(F32)

    normed_mix, parts, conv_in, conv_out, mixed, mix_part, c_edge = conv_forward(
        idx, chip_hidden, edge_rows, in_planes, out_weight, far_weights, gain_mix, taps, keeps, block
    )
    mix_came = swap_core(mix_part)
    own_x, resid_two = second_norm(chip_hidden, mix_part, mix_came, gain_ffn, 0, True)
    far_x = swap_pair(own_x)
    other_x = second_norm(tie(chip_hidden, own_x), mix_part, mix_came, gain_ffn, 1, False)[0]

    cot_other = swap_core(cot)
    cot_diag = swap_core(tie(cot_far, mix_came))
    total = 4 * rows
    act, d_gate, d_up, term_own, term_other, d_own, d_other = feed_forward(
        idx, [own_x, other_x], [cot, cot_other], weights, total, 0, ()
    )
    diag_x = swap_core(tie(far_x, d_own))
    near_d = swap_core(d_other)
    near_term = swap_core(term_other)
    act, d_gate, d_up, term_far, term_diag, d_far, d_diag = feed_forward(
        idx,
        [far_x, diag_x],
        [cot_far, cot_diag],
        weights,
        total,
        2 * rows // TILE,
        (act, d_gate, d_up),
    )
    d_diag_came = swap_core(d_diag)
    down_send, down_keep = weight_grads(
        slots_of(links), chips, [cot, cot_other, cot_far, cot_diag], [act]
    )
    sum_down = Halving(down_keep, links)
    sum_down.start(down_send)
    home = swap_pair(
        (d_far.astype(F32) + tie(d_diag_came, down_send).astype(F32)).astype(LOW)
    )
    term_home = swap_pair(
        (term_far.astype(F32) + swap_core(tie(term_diag, down_send)).astype(F32)).astype(LOW)
    )
    gate_send, gate_keep, up_send, up_keep = weight_grads(
        slots_of(turned, links), chips, [own_x, other_x, far_x, diag_x], [d_gate, tie(d_up, down_send)]
    )
    sum_gate = Halving(gate_keep, turned)
    sum_gate.start(gate_send)
    sum_up = Halving(up_keep, links)
    sum_up.start(up_send)

    d_resid, d_low, gain_ffn_terms = resid_back(d_own, near_d, home, resid_two, cot, gain_ffn)
    d_near = swap_core(d_low)
    d_head = d_low.reshape(groups, block, width)[:, :2]
    d_after = jnp.where(
        first_core,
        over_seq(d_head, [(i, i - 2) for i in even]),
        over_seq(d_head, [(i, i - 1) for i in even]),
    )
    d_edges = after_blocks(
        d_after, d_head, d_near.reshape(groups, block, width)[:, :2]
    ).reshape(4 * groups, width)
    sum_down.step(d_low)
    orders = mix_orders(links)
    slots_mix = slots_of(
        *[[0 if link == "pair" else link for link in order] for order in orders]
    )
    d_normed_own, d_normed_other, tap_terms, send_a, keep_a, send_b, keep_b = conv_back(
        idx,
        slots_mix,
        chips,
        d_low,
        d_near,
        d_edges,
        (normed_mix, parts, conv_in, conv_out, mixed, c_edge),
        in_planes,
        out_weight,
        far_weights,
        taps,
        keeps,
        block,
    )
    sum_a = Halving(keep_a, orders[0])
    sum_b = Halving(keep_b, orders[1])
    sum_a.start(send_a)
    sum_b.start(send_b)
    d_normed_came = swap_core(d_normed_other)
    sum_gate.step(send_a)
    sum_up.step(send_a)
    sum_down.step(send_a)
    grad_hidden, gain_mix_terms = hidden_back(
        d_normed_own, d_normed_came, own, d_resid, gain_mix
    )

    taps_sum = jnp.sum(tap_terms, axis=1)
    half_width = norm_mix.shape[0]
    spread = jnp.zeros((3, width), F32)
    spread = lax.dynamic_update_slice_in_dim(
        spread, taps_sum[:, :half], pair * half_width + core * half, 1
    )
    spread = lax.dynamic_update_slice_in_dim(
        spread, taps_sum[:, half:], (1 - pair) * half_width + core * half, 1
    )
    sums = jnp.concatenate(
        [
            spread,
            jnp.sum(gain_mix_terms, axis=0, keepdims=True),
            jnp.sum(gain_ffn_terms, axis=0, keepdims=True),
        ],
        axis=0,
    )
    sums = sums + swap_core(sums)
    for link in ["pair"] + links:
        sums = sums + swap(sums, link)
    sums = lax.dynamic_slice_in_dim(sums, pair * half_width, half_width, 1)
    for reduction in (sum_down, sum_gate, sum_up):
        while reduction.links:
            reduction.step(grad_hidden)
    while sum_a.links:
        sum_a.step()
        sum_b.step()

    block_out = (
        resid_two
        + (term_own.astype(F32) + near_term.astype(F32) + tie(term_home, send_a).astype(F32))
    ).astype(LOW)

    part_rows = width // size

    def finish(reductions):
        total = jnp.concatenate([reduction.done() for reduction in reductions], axis=1)
        total = total.reshape(2, part_rows, -1)
        came = swap_core(
            jnp.where(first_core, total[1], total[0]).astype(LOW)
        ).astype(F32)
        mine = jnp.where(first_core, total[0], total[1])
        each = mine.shape[1] // (3 if len(reductions) == 3 else 4)
        return [
            ordered(first_core, mine[:, at : at + each], came[:, at : at + each], 1)
            for at in range(0, mine.shape[1], each)
        ]

    out_down, out_gate, out_up = finish([sum_down, sum_gate, sum_up])
    out_out, out_b, out_c, out_x = finish([sum_a, sum_b])
    return (
        block_out.reshape(groups, block, width),
        grad_hidden.reshape(groups, block, width),
        jnp.stack([out_b, out_c, out_x], axis=1),
        out_out.T,
        out_gate,
        out_up,
        out_down.T,
        sums[:3],
        sums[3],
        sums[4],
    )


def solution(mesh):
    return jax.shard_map(
        local,
        mesh=mesh,
        in_specs=(
            P("wshard", "seq", None),
            P("wshard", "seq"),
            P("wshard", "seq", None),
            P(None, None, "wshard"),
            P("wshard", None),
            P(None, "wshard"),
            P(None, "wshard"),
            P("wshard", None),
            P(None, "wshard"),
            P("wshard"),
            P("wshard"),
        ),
        out_specs=(
            P("wshard", "seq", None),
            P("wshard", "seq", None),
            P("seq", None, "wshard"),
            P("wshard", "seq"),
            P("seq", "wshard"),
            P("seq", "wshard"),
            P("wshard", "seq"),
            P(None, "wshard"),
            P("wshard"),
            P("wshard"),
        ),
        check_vma=False,
    )
```

time: 1610 us -> 369 us (0.23)
  waiting for transfers between devices: 1180 us -> 97.9 us
  local copies, waits for them, and re-layouts: 189 us -> 15.4 us
  Pallas kernels: 0 us -> 154 us
  matrix products: 144 us -> 0 us
  blocking collectives: 54.9 us -> 0 us
  starting transfers between devices: 5.91 us -> 53.2 us
  other arithmetic: 14.2 us -> 43.8 us
    reduce_scatter x5 -> x0, waiting for transfers between devices: 762 us -> none  [the longest x1 272 us: local(): lax.psum_scatter(seq_major(grad_in, seq_size, pair_size), ('seq', 'wshard...]
    all_gather x5 -> x0, waiting for transfers between devices: 413 us -> none  [the longest x1 115 us: local(): lax.all_gather(gate_weight, 'wshard', axis=1, tiled=True)]
    pallas_call x0 -> x10, Pallas kernels: none -> 154 us  [the longest x2 66.1 us: feed_forward(): call(functools.partial(feed_forward_body, count, len(held)), 'feed_forwar...]
    dot_general x15 -> x0, matrix products: 144 us -> none  [the longest x5 48.3 us: contract_rows(): lax.dot_general(left, right, (((0,), (0,)), ((), ())), preferred_element_...]
    ppermute x3 -> x49, waiting for transfers between devices: 1.64 us -> 97.9 us  [the longest x39 64.3 us: over_seq(): return lax.ppermute(block, 'seq', route)]
    transpose x5 -> x0, local copies, waits for them, and re-layouts: 78.8 us -> none  [the longest x3 40.2 us: seq_major(): moved = jnp.moveaxis(blocked, -2, 1)]
    reshape x5 -> x1, local copies, waits for them, and re-layouts: 78.4 us -> 0.66 us  [local(): edge_rows = edges[..., :width].reshape(8 * groups, width)]
    ppermute x3 -> x49, starting transfers between devices: 5.51 us -> 53.2 us  [the longest x39 40.4 us: over_seq(): return lax.ppermute(block, 'seq', route)]
  transfers between devices with their start and end apart: 13 -> 49, of which waited for: 11 -> 16; matrix products, arithmetic and copies ran while one was open for 17% -> 14% of each run, Pallas kernels for 0% -> 28%
where the time goes in v2:
time: 369 us; the launch traced here: 366 us
  Pallas kernels  154 us (42%)
  waiting for transfers between devices  97.9 us (27%)
  starting transfers between devices  53.2 us (14%)
  other arithmetic  43.8 us (12%)
  local copies, waits for them, and re-layouts  15.4 us (4%)
    pallas_call x2, Pallas kernels, feed_forward(): call(functools.partial(feed_forward_body, count, len(held)), 'feed_forwar...  66.1 us
    ppermute x39, waiting for transfers between devices, over_seq(): return lax.ppermute(block, 'seq', route)  64.3 us
    ppermute x39, starting transfers between devices, over_seq(): return lax.ppermute(block, 'seq', route)  40.4 us
    pallas_call x2, Pallas kernels, weight_grads(): call(functools.partial(grads_body, pieces, count, chips), 'weight_grads',...  36.8 us
    ppermute x10, waiting for transfers between devices, swap_pair(): return lax.ppermute(block, 'wshard', [(0, 1), (1, 0)])  33.7 us
    pallas_call x1, Pallas kernels, conv_back(): call(functools.partial(conv_back_body, block, count, chips), 'conv_back',...  21.1 us
    convert_element_type x12, other arithmetic, step(): going = sum((term[half:2 * half].astype(F32) for term in terms)).astype(LOW)  14.4 us
    ppermute x10, starting transfers between devices, swap_pair(): return lax.ppermute(block, 'wshard', [(0, 1), (1, 0)])  12.8 us
  transfers between devices with their start and end apart: 49, of which 16 were waited for; matrix products, arithmetic and copies ran while one was open for 14% of the time, Pallas kernels for 28%

profile of v2, /device:TPU:0, one launch (start us, length us, event | category | flops | bytes accessed | tf_op | source)
XLA Modules:
  0.0 366.4 jit_solution(11778029821693012015)
XLA Ops:
  3.1 3.0 collective-permute-start.4
  10.4 19.1 %collective-permute-done.8 = bf16[5,512]{1,0:T(8,128)(2,1)S(1)} collective-permute-done((bf16[5,512]{1,0:T(8,128)(2,1)S(1)}, bf16[5,512]{1,0:T(8,128)(2,1)S(1)}, u32[]{:S(2)}, u32[]{:S(2)}) %collective-permute-start.8) | collective-permute-done | bytes 5152 | tf_op jit(solution)/shard_map/ppermute | solution.py:31
  36.6 4.5 %collective-permute-start.2 = (bf16[4,2,1152]{2,1,0:T(2,128)(2,1)S(1)}, bf16[4,2,1152]{2,1,0:T(2,128)(2,1)S(1)}, u32[]{:S(2)}, u32[]{:S(2)}) collective-permute-start(bf16[4,2,1152]{2,1,0:T(2,128)(2,1)S(1)} %get-tuple-element.150), channel_id=1, source_target_pairs={{0,4},{2,6},{4,8},{6,10},{8,12},{10,14},{12,16},{14,18},{16,20},{1... | collective-permute-start | bytes 55304 | tf_op jit(solution)/shard_map/ppermute | solution.py:19
  48.1 12.7 %conv_forward.1 = (bf16[1024,1024]{1,0:T(8,128)(2,1)}, bf16[1024,1536]{1,0:T(8,128)(2,1)}, bf16[1024,512]{1,0:T(8,128)(2,1)}, bf16[1024,512]{1,0:T(8,128)(2,1)},...) custom-call(s32[2]{0:T(128)} %pad_add_fusion.1.idx, ...), custom_call_target="tpu_custom_call" | custom-call | flops 1000 | bytes 1000 | tf_op jit(solution)/shard_map/conv_forward/pallas_call | solution.py:195
  66.6 4.3 %second_norm.2 = (bf16[512,1024]{1,0:T(8,128)(2,1)}, f32[512,1024]{1,0:T(8,128)}) custom-call(bf16[1024,1024]{1,0:T(8,128)(2,1)} %pad_maximum_fusion.x_ref, bf16[1024,1024]{1,0:T(8,128)(2,1)} %get-tuple-element.71.mine_ref, bf16[1024,1024]{1,0:T(8,128)(2,1)} %copy-done.2, f32[1,1024]{1,0:T(1,128)} %get-tuple-element.157.gain_ref), custom_call_target="tpu_custom_call" | custom-call | flops 1000 | bytes 1000 | tf_op jit(solution)/shard_map/second_norm/pallas_call | solution.py:249
  72.4 14.6 %collective-permute-done.14.refs_2_ = bf16[512,1024]{1,0:T(8,128)(2,1)S(1)} collective-permute-done((bf16[512,1024]{1,0:T(8,128)(2,1)S(1)}, bf16[512,1024]{1,0:T(8,128)(2,1)S(1)}, u32[]{:S(2)}, u32[]{:S(2)}) %collective-permute-start.14) | collective-permute-done | bytes 1048608 | tf_op jit(solution)/shard_map/ppermute | solution.py:31
  87.0 4.5 %second_norm.3.refs_1_ = bf16[512,1024]{1,0:T(8,128)(2,1)} custom-call(bf16[1024,1024]{1,0:T(8,128)(2,1)} %pad_maximum_fusion.x_ref, bf16[1024,1024]{1,0:T(8,128)(2,1)} %get-tuple-element.71.mine_ref, bf16[1024,1024]{1,0:T(8,128)(2,1)} %copy-done.2, f32[1,1024]{1,0:T(1,128)} %get-tuple-element.157.gain_ref), custom_call_target="tpu_custom_call" | custom-call | flops 1000 | bytes 1000 | tf_op jit(solution)/shard_map/second_norm/pallas_call | solution.py:249
  92.4 27.2 %feed_forward.2 = (bf16[2048,1152]{1,0:T(8,128)(2,1)}, bf16[2048,1152]{1,0:T(8,128)(2,1)}, bf16[2048,1152]{1,0:T(8,128)(2,1)}, bf16[512,1024]{1,0:T(8,128)(2,1)}...) custom-call(s32[2]{0:T(128)} %pad_add_fusion.1.idx, ...), custom_call_target="tpu_custom_call" | custom-call | flops 1000 | bytes 1000 | tf_op jit(solution)/shard_map/feed_forward/pallas_call | solution.py:332
  123.4 38.9 %feed_forward.3 = (bf16[2048,1152]{1,0:T(8,128)(2,1)}, bf16[2048,1152]{1,0:T(8,128)(2,1)}, bf16[2048,1152]{1,0:T(8,128)(2,1)}, bf16[512,1024]{1,0:T(8,128)(2,1)}...) custom-call(s32[2]{0:T(128)} %pad_add_fusion.1.idx, ...), custom_call_target="tpu_custom_call", output_to_operand_aliasing={{0}: (8, {}), {1}: (9, {}), {2}: (10, {})} | custom-call | flops 1000 | bytes 1000 | tf_op jit(solution)/shard_map/feed_forward/pallas_call | solution.py:332
  163.4 12.0 %weight_grads.2 = (bf16[4,128,1152]{2,1,0:T(8,128)(2,1)}, bf16[4,128,1152]{2,1,0:T(8,128)(2,1)}) custom-call(s32[8]{0:T(128)} %broadcast_xor_fusion.2.slots, bf16[512,1024]{1,0:T(8,128)(2,1)} %bitcast.72, bf16[512,1024]{1,0:T(8,128)(2,1)} %copy-done.8, bf16[512,1024]{1,0:T(8,128)(2,1)} %copy-done.4, bf16[512,1024]{1,0:T(8,128)(2,1)} %copy-done.5, ...), custom_call_target="tpu_custom_call" | custom-call | flops 1000 | bytes 1000 | tf_op jit(solution)/shard_map/weight_grads/pallas_call | solution.py:407
  177.3 2.7 collective-permute-start.34
  181.1 24.8 %weight_grads.3 = (bf16[4,128,1152]{2,1,0:T(8,128)(2,1)}, bf16[4,128,1152]{2,1,0:T(8,128)(2,1)}, bf16[4,128,1152]{2,1,0:T(8,128)(2,1)}, bf16[4,128,1152]{2,1,0:T(8,128)(2,1)}) custom-call(s32[16]{0:T(128)} %broadcast_xor_fusion.slots, bf16[512,1024]{1,0:T(8,128)(2,1)} %get-tuple-element.73.refs_0_, bf16[512,1024]{1,0:T(8,128)(2,1)} %second_norm.3.refs_1_, ...), custom_call_target="tpu_custom_call" | custom-call | flops 1000 | bytes 1000 | tf_op jit(solution)/shard_map/weight_grads/pallas_call | solution.py:407
  206.0 4.8 %resid_back.1 = (f32[512,1024]{1,0:T(8,128)}, bf16[512,1024]{1,0:T(8,128)(2,1)}, f32[8,1024]{1,0:T(8,128)}) custom-call(bf16[512,1024]{1,0:T(8,128)(2,1)} %get-tuple-element.77.mine_ref, bf16[512,1024]{1,0:T(8,128)(2,1)} %collective-permute-done.18.near_ref, bf16[512,1024]{1,0:T(8,128)(2,1)} %collective-permute-done.20.far_ref, ...), custom_call_target="tpu_custom_call" | custom-call | flops 1000 | bytes 1000 | tf_op jit(solution)/shard_map/resid_back/pallas_call | solution.py:459
  216.4 4.5 %collective-permute-start.35 = (bf16[2,128,1152]{2,1,0:T(8,128)(2,1)}, bf16[2,128,1152]{2,1,0:T(8,128)(2,1)}, u32[]{:S(2)}, u32[]{:S(2)}) collective-permute-start(bf16[2,128,1152]{2,1,0:T(8,128)(2,1)} %add_convert_fusion.5), channel_id=1, source_target_pairs={{0,8},{2,10},{4,12},{6,14},{8,0},{10,2},{12,4},{14,6},{16,24},{18,... | collective-permute-start | bytes 1769480 | tf_op jit(solution)/shard_map/ppermute | solution.py:19
  224.8 10.1 %collective-permute-done.22 = bf16[4,2,1024]{2,1,0:T(2,128)(2,1)} collective-permute-done((bf16[4,2,1024]{2,1,0:T(2,128)(2,1)}, bf16[4,2,1024]{2,1,0:T(2,128)(2,1)}, u32[]{:S(2)}, u32[]{:S(2)}) %collective-permute-start.22) | collective-permute-done | bytes 16416 | tf_op jit(solution)/shard_map/ppermute | solution.py:19
  238.6 21.1 %conv_back.1 = (bf16[512,1024]{1,0:T(8,128)(2,1)}, bf16[512,1024]{1,0:T(8,128)(2,1)}, f32[3,8,512]{2,1,0:T(8,128)}, bf16[8,128,512]{2,1,0:T(8,128)(2,1)}, bf16[8...) custom-call(s32[2]{0:T(128)} %pad_add_fusion.1.idx, ...), custom_call_target="tpu_custom_call" | custom-call | flops 1000 | bytes 1000 | tf_op jit(solution)/shard_map/conv_back/pallas_call | solution.py:635
  265.4 3.3 add_convert_fusion
  277.6 4.1 %hidden_back.1 = (f32[512,1024]{1,0:T(8,128)}, f32[8,1024]{1,0:T(8,128)}) custom-call(bf16[512,1024]{1,0:T(8,128)(2,1)} %get-tuple-element.102.mine_ref, bf16[512,1024]{1,0:T(8,128)(2,1)} %collective-permute-done.24.came_ref, bf16[512,1024]{1,0:T(8,128)(2,1)} %bitcast.76, f32[512,1024]{1,0:T(8,128)} %get-tuple-element.104.d_ref, ...), custom_call_target="tpu_custom_call" | custom-call | flops 1000 | bytes 1000 | tf_op jit(solution)/shard_map/hidden_back/pallas_call | solution.py:714
  294.7 8.1 %collective-permute-done.46 = f32[5,1024]{1,0:T(8,128)S(1)} collective-permute-done((f32[5,1024]{1,0:T(8,128)S(1)}, f32[5,1024]{1,0:T(8,128)S(1)}, u32[]{:S(2)}, u32[]{:S(2)}) %collective-permute-start.46) | collective-permute-done | bytes 20512 | tf_op jit(solution)/shard_map/ppermute | solution.py:19
  311.9 16.8 %collective-permute-done.48 = f32[5,1024]{1,0:T(8,128)S(1)} collective-permute-done((f32[5,1024]{1,0:T(8,128)S(1)}, f32[5,1024]{1,0:T(8,128)S(1)}, u32[]{:S(2)}, u32[]{:S(2)}) %collective-permute-start.48) | collective-permute-done | bytes 20512 | tf_op jit(solution)/shard_map/ppermute | solution.py:19
  331.0 3.3 collective-permute-done.39
  342.3 3.8 %collective-permute-done.31 = bf16[2,128,512]{2,1,0:T(8,128)(2,1)S(1)} collective-permute-done((bf16[2,128,512]{2,1,0:T(8,128)(2,1)S(1)}, bf16[2,128,512]{2,1,0:T(8,128)(2,1)S(1)}, u32[]{:S(2)}, u32[]{:S(2)}) %collective-permute-start.31) | collective-permute-done | bytes 262176 | tf_op jit(solution)/shard_map/ppermute | solution.py:19
  348.3 5.0 %collective-permute-done.27 = bf16[2,128,512]{2,1,0:T(8,128)(2,1)S(1)} collective-permute-done((bf16[2,128,512]{2,1,0:T(8,128)(2,1)S(1)}, bf16[2,128,512]{2,1,0:T(8,128)(2,1)S(1)}, u32[]{:S(2)}, u32[]{:S(2)}) %collective-permute-start.27) | collective-permute-done | bytes 262176 | tf_op jit(solution)/shard_map/ppermute | solution.py:19
  356.8 5.3 %collective-permute-done.28 = bf16[1,128,512]{2,1,0:T(8,128)(2,1)S(1)} collective-permute-done((bf16[1,128,512]{2,1,0:T(8,128)(2,1)S(1)}, bf16[1,128,512]{2,1,0:T(8,128)(2,1)S(1)}, u32[]{:S(2)}, u32[]{:S(2)}) %collective-permute-start.28) | collective-permute-done | bytes 131104 | tf_op jit(solution)/shard_map/ppermute | solution.py:19
  (254 shorter events, 106.3 us)
Async XLA Ops:
  3.1 27.6 %collective-permute-start.4 = (bf16[4,256,256]{2,1,0:T(8,128)(2,1)S(1)}, bf16[4,256,256]{2,1,0:T(8,128)(2,1)S(1)}, u32[]{:S(2)}, u32[]{:S(2)}) collective-permute-start(bf16[4,256,256]{2,1,0:T(8,128)(2,1)S(1)} %pad_maximum_fusion.2), channel_id=1, source_target_pairs={{0,1},{1,0},{2,3},{3,2},{4,5},{5,4},{6,7},{7,6},{8,9},{9,8},{10,11... | collective-permute-start | bytes 1572872 | tf_op jit(solution)/shard_map/ppermute | solution.py:31
  6.9 39.9 %collective-permute-start.7 = (bf16[4,256,256]{2,1,0:T(8,128)(2,1)}, bf16[4,256,256]{2,1,0:T(8,128)(2,1)S(1)}, u32[]{:S(2)}, u32[]{:S(2)}) collective-permute-start(bf16[4,256,256]{2,1,0:T(8,128)(2,1)} %pad_maximum_fusion.3), channel_id=1, source_target_pairs={{0,1},{1,0},{2,3},{3,2},{4,5},{5,4},{6,7},{7,6},{8,9},{9,8},{10,11... | collective-permute-start | bytes 1572872 | tf_op jit(solution)/shard_map/ppermute | solution.py:31
  7.0 27.0 %collective-permute-start = (bf16[512,1024]{1,0:T(8,128)(2,1)S(1)}, bf16[512,1024]{1,0:T(8,128)(2,1)}, u32[]{:S(2)}, u32[]{:S(2)}) collective-permute-start(bf16[512,1024]{1,0:T(8,128)(2,1)S(1)} %bitcast.77), channel_id=1, source_target_pairs={{0,2},{2,0},{4,6},{6,4},{8,10},{10,8},{12,14},{14,12},{16,18},{18,... | collective-permute-start | bytes 3145736 | tf_op jit(solution)/shard_map/ppermute | solution.py:19
  60.9 26.0 %collective-permute-start.14 = (bf16[512,1024]{1,0:T(8,128)(2,1)S(1)}, bf16[512,1024]{1,0:T(8,128)(2,1)S(1)}, u32[]{:S(2)}, u32[]{:S(2)}) collective-permute-start(bf16[512,1024]{1,0:T(8,128)(2,1)S(1)} %bitcast.74), channel_id=1, source_target_pairs={{0,1},{1,0},{2,3},{3,2},{4,5},{5,4},{6,7},{7,6},{8,9},{9,8},{10,11... | collective-permute-start | bytes 3145736 | tf_op jit(solution)/shard_map/ppermute | solution.py:31
  62.4 29.0 %collective-permute-start.10 = (bf16[512,1024]{1,0:T(8,128)(2,1)S(1)}, bf16[512,1024]{1,0:T(8,128)(2,1)S(1)}, u32[]{:S(2)}, u32[]{:S(2)}) collective-permute-start(bf16[512,1024]{1,0:T(8,128)(2,1)S(1)} %bitcast.75), channel_id=1, source_target_pairs={{0,2},{2,0},{4,6},{6,4},{8,10},{10,8},{12,14},{14,12},{16,18},{18,... | collective-permute-start | bytes 3145736 | tf_op jit(solution)/shard_map/ppermute | solution.py:19
  71.0 48.7 %collective-permute-start.12 = (bf16[512,1024]{1,0:T(8,128)(2,1)}, bf16[512,1024]{1,0:T(8,128)(2,1)S(1)}, u32[]{:S(2)}, u32[]{:S(2)}) collective-permute-start(bf16[512,1024]{1,0:T(8,128)(2,1)} %get-tuple-element.73.refs_0_), channel_id=1, source_target_pairs={{0,1},{1,0},{2,3},{3,2},{4,5},{5,4},{6,7},{7,6},{8,9},{9,8},{10,11... | collective-permute-start | bytes 3145736 | tf_op jit(solution)/shard_map/ppermute | solution.py:31
  86.9 32.9 %collective-permute-start.15 = (bf16[512,1024]{1,0:T(8,128)(2,1)S(1)}, bf16[512,1024]{1,0:T(8,128)(2,1)S(1)}, u32[]{:S(2)}, u32[]{:S(2)}) collective-permute-start(bf16[512,1024]{1,0:T(8,128)(2,1)S(1)} %collective-permute-done.14.refs_2_), channel_id=1, source_target_pairs={{0,2},{2,0},{4,6},{6,4},{8,10},{10,8},{12,14},{14,12},{16,18},{18,... | collective-permute-start | bytes 3145736 | tf_op jit(solution)/shard_map/ppermute | solution.py:19
  163.0 43.0 %collective-permute-start.18 = (bf16[512,1024]{1,0:T(8,128)(2,1)}, bf16[512,1024]{1,0:T(8,128)(2,1)}, u32[]{:S(2)}, u32[]{:S(2)}) collective-permute-start(bf16[512,1024]{1,0:T(8,128)(2,1)} %get-tuple-element.89), channel_id=1, source_target_pairs={{0,2},{2,0},{4,6},{6,4},{8,10},{10,8},{12,14},{14,12},{16,18},{18,... | collective-permute-start | bytes 3145736 | tf_op jit(solution)/shard_map/ppermute | solution.py:19
  175.9 30.2 %collective-permute-start.20 = (bf16[512,1024]{1,0:T(8,128)(2,1)S(1)}, bf16[512,1024]{1,0:T(8,128)(2,1)}, u32[]{:S(2)}, u32[]{:S(2)}) collective-permute-start(bf16[512,1024]{1,0:T(8,128)(2,1)S(1)} %add_convert_fusion.1), channel_id=1, source_target_pairs={{0,1},{1,0},{2,3},{3,2},{4,5},{5,4},{6,7},{7,6},{8,9},{9,8},{10,11... | collective-permute-start | bytes 3145736 | tf_op jit(solution)/shard_map/ppermute | solution.py:31
  177.3 36.8 %collective-permute-start.34 = (bf16[4,128,1152]{2,1,0:T(8,128)(2,1)}, bf16[4,128,1152]{2,1,0:T(8,128)(2,1)S(1)}, u32[]{:S(2)}, u32[]{:S(2)}) collective-permute-start(bf16[4,128,1152]{2,1,0:T(8,128)(2,1)} %get-tuple-element.87), channel_id=1, source_target_pairs={{0,4},{2,6},{4,0},{6,2},{8,12},{10,14},{12,8},{14,10},{16,20},{18,... | collective-permute-start | bytes 3538952 | tf_op jit(solution)/shard_map/ppermute | solution.py:19
  180.1 36.3 %collective-permute-start.16 = (bf16[512,1024]{1,0:T(8,128)(2,1)}, bf16[512,1024]{1,0:T(8,128)(2,1)}, u32[]{:S(2)}, u32[]{:S(2)}) collective-permute-start(bf16[512,1024]{1,0:T(8,128)(2,1)} %get-tuple-element.88), channel_id=1, source_target_pairs={{0,2},{2,0},{4,6},{6,4},{8,10},{10,8},{12,14},{14,12},{16,18},{18,... | collective-permute-start | bytes 3145736 | tf_op jit(solution)/shard_map/ppermute | solution.py:19
  205.9 57.3 %collective-permute-start.40 = (bf16[4,128,1152]{2,1,0:T(8,128)(2,1)}, bf16[4,128,1152]{2,1,0:T(8,128)(2,1)S(1)}, u32[]{:S(2)}, u32[]{:S(2)}) collective-permute-start(bf16[4,128,1152]{2,1,0:T(8,128)(2,1)} %get-tuple-element.120), channel_id=1, source_target_pairs={{0,4},{2,6},{4,0},{6,2},{8,12},{10,14},{12,8},{14,10},{16,20},{18,... | collective-permute-start | bytes 3538952 | tf_op jit(solution)/shard_map/ppermute | solution.py:19
  210.8 25.3 %collective-permute-start.21 = (bf16[512,1024]{1,0:T(8,128)(2,1)}, bf16[512,1024]{1,0:T(8,128)(2,1)}, u32[]{:S(2)}, u32[]{:S(2)}) collective-permute-start(bf16[512,1024]{1,0:T(8,128)(2,1)} %get-tuple-element.93.own_ref), channel_id=1, source_target_pairs={{0,2},{2,0},{4,6},{6,4},{8,10},{10,8},{12,14},{14,12},{16,18},{18,... | collective-permute-start | bytes 3145736 | tf_op jit(solution)/shard_map/ppermute | solution.py:19
  216.4 43.3 %collective-permute-start.35 = (bf16[2,128,1152]{2,1,0:T(8,128)(2,1)}, bf16[2,128,1152]{2,1,0:T(8,128)(2,1)}, u32[]{:S(2)}, u32[]{:S(2)}) collective-permute-start(bf16[2,128,1152]{2,1,0:T(8,128)(2,1)} %add_convert_fusion.5), channel_id=1, source_target_pairs={{0,8},{2,10},{4,12},{6,14},{8,0},{10,2},{12,4},{14,6},{16,24},{18,... | collective-permute-start | bytes 1769480 | tf_op jit(solution)/shard_map/ppermute | solution.py:19
  234.9 29.4 %collective-permute-start.11 = (bf16[512,1024]{1,0:T(8,128)(2,1)}, bf16[512,1024]{1,0:T(8,128)(2,1)}, u32[]{:S(2)}, u32[]{:S(2)}) collective-permute-start(bf16[512,1024]{1,0:T(8,128)(2,1)} %get-tuple-element.76), channel_id=1, source_target_pairs={{0,2},{2,0},{4,6},{6,4},{8,10},{10,8},{12,14},{14,12},{16,18},{18,... | collective-permute-start | bytes 3145736 | tf_op jit(solution)/shard_map/ppermute | solution.py:19
  234.9 28.3 %collective-permute-start.17 = (bf16[512,1024]{1,0:T(8,128)(2,1)}, bf16[512,1024]{1,0:T(8,128)(2,1)}, u32[]{:S(2)}, u32[]{:S(2)}) collective-permute-start(bf16[512,1024]{1,0:T(8,128)(2,1)} %add_convert_fusion.2), channel_id=1, source_target_pairs={{0,1},{1,0},{2,3},{3,2},{4,5},{5,4},{6,7},{7,6},{8,9},{9,8},{10,11... | collective-permute-start | bytes 3145736 | tf_op jit(solution)/shard_map/ppermute | solution.py:31
  236.1 34.8 %collective-permute-start.37 = (bf16[4,128,1152]{2,1,0:T(8,128)(2,1)}, bf16[4,128,1152]{2,1,0:T(8,128)(2,1)}, u32[]{:S(2)}, u32[]{:S(2)}) collective-permute-start(bf16[4,128,1152]{2,1,0:T(8,128)(2,1)} %get-tuple-element.116), channel_id=1, source_target_pairs={{0,8},{2,10},{4,12},{6,14},{8,0},{10,2},{12,4},{14,6},{16,24},{18,... | collective-permute-start | bytes 3538952 | tf_op jit(solution)/shard_map/ppermute | solution.py:19
  259.7 32.7 %collective-permute-start.25 = (bf16[8,128,512]{2,1,0:T(8,128)(2,1)}, bf16[8,128,512]{2,1,0:T(8,128)(2,1)}, u32[]{:S(2)}, u32[]{:S(2)}) collective-permute-start(bf16[8,128,512]{2,1,0:T(8,128)(2,1)} %get-tuple-element.100), channel_id=1, source_target_pairs={{0,1},{1,0},{2,3},{3,2},{4,5},{5,4},{6,7},{7,6},{8,9},{9,8},{10,11... | collective-permute-start | bytes 3145736 | tf_op jit(solution)/shard_map/ppermute | solution.py:31
  263.2 26.3 %collective-permute-start.29 = (bf16[8,128,512]{2,1,0:T(8,128)(2,1)}, bf16[8,128,512]{2,1,0:T(8,128)(2,1)}, u32[]{:S(2)}, u32[]{:S(2)}) collective-permute-start(bf16[8,128,512]{2,1,0:T(8,128)(2,1)} %get-tuple-element.108), channel_id=1, source_target_pairs={{0,4},{2,6},{4,0},{6,2},{8,12},{10,14},{12,8},{14,10},{16,20},{18,... | collective-permute-start | bytes 3145736 | tf_op jit(solution)/shard_map/ppermute | solution.py:19
  264.2 39.7 %collective-permute-start.41 = (bf16[2,128,1152]{2,1,0:T(8,128)(2,1)}, bf16[2,128,1152]{2,1,0:T(8,128)(2,1)}, u32[]{:S(2)}, u32[]{:S(2)}) collective-permute-start(bf16[2,128,1152]{2,1,0:T(8,128)(2,1)} %add_convert_fusion.3), channel_id=1, source_target_pairs={{0,8},{2,10},{4,12},{6,14},{8,0},{10,2},{12,4},{14,6},{16,24},{18,... | collective-permute-start | bytes 1769480 | tf_op jit(solution)/shard_map/ppermute | solution.py:19
  275.5 33.7 %collective-permute-start.38 = (bf16[2,128,1152]{2,1,0:T(8,128)(2,1)}, bf16[2,128,1152]{2,1,0:T(8,128)(2,1)}, u32[]{:S(2)}, u32[]{:S(2)}) collective-permute-start(bf16[2,128,1152]{2,1,0:T(8,128)(2,1)} %add_convert_fusion.4), channel_id=1, source_target_pairs={{0,4},{2,6},{4,0},{6,2},{8,12},{10,14},{12,8},{14,10},{16,20},{18,... | collective-permute-start | bytes 1769480 | tf_op jit(solution)/shard_map/ppermute | solution.py:19
  290.7 45.2 %collective-permute-start.30 = (bf16[4,128,512]{2,1,0:T(8,128)(2,1)S(1)}, bf16[4,128,512]{2,1,0:T(8,128)(2,1)S(1)}, u32[]{:S(2)}, u32[]{:S(2)}) collective-permute-start(bf16[4,128,512]{2,1,0:T(8,128)(2,1)S(1)} %add_convert_fusion.6), channel_id=1, source_target_pairs={{0,1},{1,0},{2,3},{3,2},{4,5},{5,4},{6,7},{7,6},{8,9},{9,8},{10,11... | collective-permute-start | bytes 1572872 | tf_op jit(solution)/shard_map/ppermute | solution.py:31
  293.6 43.5 %collective-permute-start.26 = (bf16[4,128,512]{2,1,0:T(8,128)(2,1)S(1)}, bf16[4,128,512]{2,1,0:T(8,128)(2,1)S(1)}, u32[]{:S(2)}, u32[]{:S(2)}) collective-permute-start(bf16[4,128,512]{2,1,0:T(8,128)(2,1)S(1)} %add_convert_fusion.7), channel_id=1, source_target_pairs={{0,4},{2,6},{4,0},{6,2},{8,12},{10,14},{12,8},{14,10},{16,20},{18,... | collective-permute-start | bytes 1572872 | tf_op jit(solution)/shard_map/ppermute | solution.py:19
  305.0 24.9 %collective-permute-start.42 = (bf16[1,128,1152]{2,1,0:T(8,128)(2,1)S(1)}, bf16[1,128,1152]{2,1,0:T(8,128)(2,1)S(1)}, u32[]{:S(2)}, u32[]{:S(2)}) collective-permute-start(bf16[1,128,1152]{2,1,0:T(8,128)(2,1)S(1)} %add_convert_fusion.8), channel_id=1, source_target_pairs={{0,16},{2,18},{4,20},{6,22},{8,24},{10,26},{12,28},{14,30},{16,0},... | collective-permute-start | bytes 884744 | tf_op jit(solution)/shard_map/ppermute | solution.py:19
  (57 other events, 528.5 us)

commit v3 on v2

--- a/solution.py
+++ b/solution.py
@@ -51,7 +51,9 @@
     return lax.dot_general(left, right, TN, preferred_element_type=F32)
 
 
-def call(body, name, grid, in_specs, out_specs, out_shape, scratch=(), scalars=1, aliases=None):
+def call(
+    body, name, grid, in_specs, out_specs, out_shape, scratch=(), scalars=1, aliases=None, mib=36
+):
     return pl.pallas_call(
         body,
         grid_spec=pltpu.PrefetchScalarGridSpec(
@@ -63,7 +65,7 @@
         ),
         out_shape=out_shape,
         input_output_aliases=aliases or {},
-        compiler_params=pltpu.CompilerParams(vmem_limit_bytes=56 * 2**20),
+        compiler_params=pltpu.CompilerParams(vmem_limit_bytes=mib * 2**20),
         cost_estimate=pl.CostEstimate(flops=1000, bytes_accessed=1000, transcendentals=0),
         name=name,
     )
@@ -107,7 +109,8 @@
     conv_in_ref,
     conv_out_ref,
     mixed_ref,
-    mix_ref,
+    own_mix_ref,
+    other_mix_ref,
     c_edge_ref,
     nx,
     edge_in,
@@ -179,7 +182,16 @@
     for p in range(4):
         where = piece_columns(place, p, depth)
         acc[:, where] += dot(mixed[:, half:], far[p][3])
-    mix_ref[...] = acc[...].astype(LOW)
+    mix = acc[...].astype(LOW)
+    count = pl.num_programs(0) // 2
+
+    @pl.when(step < count)
+    def _():
+        own_mix_ref[...] = mix
+
+    @pl.when(step >= count)
+    def _():
+        other_mix_ref[...] = mix
 
 
 def conv_forward(idx, x, edges, in_weight, out_weight, far, gain, taps, keeps, block):
@@ -192,6 +204,7 @@
         return pl.BlockSpec((rows, columns), lambda i, s: (i, 0))
 
     before = edges.shape[0] // 2
+    count = total // rows // 2
     return call(
         functools.partial(conv_forward_body, block),
         "conv_forward",
@@ -212,16 +225,18 @@
             rowed(cols),
             rowed(cols),
             rowed(cols),
-            rowed(width),
+            pl.BlockSpec((rows, width), lambda i, s: (jnp.minimum(i, count - 1), 0)),
+            pl.BlockSpec((rows, width), lambda i, s: (jnp.maximum(i - count, 0), 0)),
             pl.BlockSpec((before, cols), lambda i, s: (0, 0)),
         ],
         [
-            shape(total, width),
-            shape(total, 3 * cols),
-            shape(total, cols),
-            shape(total, cols),
-            shape(total, cols),
-            shape(total, width),
+            pltpu.HBM((total, width), LOW),
+            pltpu.HBM((total, 3 * cols), LOW),
+            pltpu.HBM((total, cols), LOW),
+            pltpu.HBM((total, cols), LOW),
+            pltpu.HBM((total, cols), LOW),
+            shape(total // 2, width),
+            shape(total // 2, width),
             shape(before, cols, F32),
         ],
         [
@@ -240,7 +255,7 @@
 
 
 def second_norm(x, mine, came, gain, which, keep):
-    rows, width = x.shape[0] // 2, x.shape[1]
+    rows, width = mine.shape
     tile = rows // 4
 
     def plain(start):
@@ -250,45 +265,25 @@
         second_norm_body,
         "second_norm",
         (4,),
-        [plain(which), plain(which), plain(1 - which), whole(gain)],
+        [plain(which), plain(0), plain(0), whole(gain)],
         [plain(0)] * (1 + keep),
-        [shape(rows, width), shape(rows, width, F32)][: 1 + keep],
+        [shape(rows, width), pltpu.HBM((rows, width), F32)][: 1 + keep],
         scalars=0,
+        mib=12,
     )(x, mine, came, gain)
 
 
 def feed_forward_body(count, held, idx, *refs):
     x_refs, ct_refs = refs[:2], refs[2:4]
-    gate_hbm, up_hbm, down_hbm = refs[4:7]
+    gate_ref, up_ref, down_ref = refs[4:7]
     refs = refs[7 + held :]
-    act_ref, d_gate_ref, d_up_ref, term_a, term_b, d_a, d_b, gate_ref, up_ref, down_ref, sems = refs
+    act_ref, d_gate_ref, d_up_ref, term_a, term_b, d_a, d_b = refs
     step = pl.program_id(0)
     first = step < count
-    units = gate_ref.shape[1]
-    mine = pl.ds(pl.multiple_of(idx[0] * units, 128), units)
-    copies = [
-        pltpu.make_async_copy(gate_hbm.at[:, mine], gate_ref, sems.at[0]),
-        pltpu.make_async_copy(up_hbm.at[:, mine], up_ref, sems.at[1]),
-        pltpu.make_async_copy(down_hbm.at[mine, :], down_ref, sems.at[2]),
-    ]
-
-    def there(copy):
-        @pl.when(step == 0)
-        def _():
-            copy.wait()
-
-    @pl.when(step == 0)
-    def _():
-        for copy in copies:
-            copy.start()
-
     x = jnp.where(first, x_refs[0][...], x_refs[1][...])
     upstream = jnp.where(first, ct_refs[0][...], ct_refs[1][...])
-    there(copies[0])
     gate = dot(x, gate_ref[...])
-    there(copies[1])
     up_value = dot(x, up_ref[...])
-    there(copies[2])
     d_act = dot_nt(upstream, down_ref[...])
     sigma = jax.nn.sigmoid(gate)
     silu_gate = gate * sigma
@@ -329,20 +324,18 @@
 
     any_spec = pl.BlockSpec(memory_space=pl.ANY)
     unit_spec = pl.BlockSpec((TILE, units), lambda i, s: (i + start, 0))
+    columns = pl.BlockSpec((width, units), lambda i, s: (0, s[0]))
     return call(
         functools.partial(feed_forward_body, count, len(held)),
         "feed_forward",
         (2 * count,),
-        [rowed(lower), rowed(upper)] * 2 + [any_spec] * (3 + len(held)),
+        [rowed(lower), rowed(upper)] * 2
+        + [columns, columns, pl.BlockSpec((units, width), lambda i, s: (s[0], 0))]
+        + [any_spec] * len(held),
         [unit_spec] * 3 + [rowed(lower), rowed(upper)] * 2,
         [shape(total, units)] * 3 + [shape(rows, width)] * 4,
-        [
-            pltpu.VMEM((width, units), LOW),
-            pltpu.VMEM((width, units), LOW),
-            pltpu.VMEM((units, width), LOW),
-            pltpu.SemaphoreType.DMA((3,)),
-        ],
         aliases={8 + k: k for k in range(len(held))},
+        mib=30,
     )(idx, *xs, *cts, gate, up, down, *held)
 
 
@@ -381,6 +374,7 @@
             if a == 0:
                 x_copy(k).wait()
             y_copy(a, k).wait()
+        for k in range(pieces):
             term = dot_tn(x_buf[k], y_buf[a, k])
             if k == 0:
                 acc[...] = term
@@ -420,6 +414,7 @@
             pltpu.SemaphoreType.DMA((count, pieces)),
             pltpu.SemaphoreType.DMA((count, 2)),
         ],
+        mib=26,
     )(slots, *xs, *ys)
 
 
@@ -464,6 +459,7 @@
         [plain(), plain(), pl.BlockSpec((8, width), lambda i: (0, 0))],
         [shape(rows, width, F32), shape(rows, width), shape(8, width, F32)],
         scalars=0,
+        mib=16,
     )(mine, near, far, two, cot, gain)
 
 
@@ -476,6 +472,8 @@
     own_ref,
     other_ref,
     edge_ref,
+    x_ref,
+    gain_terms_ref,
     normed_ref,
     mixed_ref,
     parts_ref,
@@ -492,7 +490,7 @@
     keep_ref,
     own_normed_ref,
     other_normed_ref,
-    taps_out_ref,
+    sums_ref,
     send_a,
     keep_a,
     send_b,
@@ -503,6 +501,8 @@
     d_proj,
     in_acc,
     out_acc,
+    taps_acc,
+    gain_acc,
     bufs,
     sems,
 ):
@@ -526,7 +526,8 @@
         edge_d[...] = back_out(lambda columns: edge_ref[:, columns]) * c_edge_ref[...]
         in_acc[...] = jnp.zeros_like(in_acc)
         out_acc[...] = jnp.zeros_like(out_acc)
-        taps_out_ref[...] = jnp.zeros_like(taps_out_ref)
+        taps_acc[...] = jnp.zeros_like(taps_acc)
+        gain_acc[...] = jnp.zeros_like(gain_acc)
 
     held[...] = jnp.where(step < count, own_ref[...], other_ref[...])
     d_mixed = back_out(lambda columns: held[:, columns])
@@ -551,7 +552,7 @@
         d_in = taps_ref[2:3, :] * here + taps_ref[1:2, :] * next_one + taps_ref[0:1, :] * next_two
         conv_in = conv_in_ref[span, :].astype(F32)
         for k, term in enumerate((next_two, next_one, here)):
-            taps_out_ref[k] += jnp.sum((term * conv_in).reshape(-1, 8, cols), axis=0)
+            taps_acc[k] += jnp.sum((term * conv_in).reshape(-1, 8, cols), axis=0)
         d_proj[span, :cols] = (d_in * parts_ref[span, 2 * cols :].astype(F32)).astype(LOW)
         d_proj[span, 2 * cols :] = (d_in * parts_ref[span, :cols].astype(F32)).astype(LOW)
     out_acc[...] += dot_tn(held[...], mixed_ref[...])
@@ -568,6 +569,10 @@
             term = dot_nt(d_proj[:, j * cols + half : (j + 1) * cols], far[p][j])
             total = term if total is None else total + term
         acc[:, where] += total
+    wide = x_ref[...].astype(F32)
+    scale = lax.rsqrt(jnp.mean(wide * wide, axis=-1, keepdims=True) + EPS)
+    terms = acc[...] * (wide * scale)
+    gain_acc[...] += jnp.sum(terms.reshape(-1, 8, terms.shape[1]), axis=0)
 
     @pl.when(step < count)
     def _():
@@ -579,6 +584,15 @@
 
     @pl.when(step == 2 * count - 1)
     def _():
+        sums_ref[...] = jnp.zeros_like(sums_ref)
+        for k in range(3):
+            line = jnp.sum(taps_acc[k], axis=0, keepdims=True)
+            for part in range(2):
+                side = idx[2] if part == 0 else 1 - idx[2]
+                at = pl.multiple_of((2 * side + idx[0]) * half, 128)
+                sums_ref[k : k + 1, pl.ds(at, half)] = line[:, part * half : (part + 1) * half]
+        sums_ref[3:4, :] = jnp.sum(gain_acc[...], axis=0, keepdims=True)
+        sums_ref[4:5, :] = jnp.sum(gain_terms_ref[...], axis=0, keepdims=True)
         rows = in_acc.shape[0] // chips
         copies = []
         for a, (halves, keeps, sends) in enumerate(
@@ -613,7 +627,7 @@
     return ["pair"] + links, [links[0], "pair"] + links[1:]
 
 
-def conv_back(idx, slots, chips, own, other, edges, kept, in_weight, out_weight, far, taps, keeps, block):
+def conv_back(idx, slots, chips, own, other, edges, x, gain_terms, kept, in_weight, out_weight, far, taps, keeps, block):
     normed_mix, parts, conv_in, conv_out, mixed, c_edge = kept
     rows, width = own.shape
     half = far[0].shape[2]
@@ -641,6 +655,8 @@
             upper,
             fixed(edges),
             rowed(width),
+            fixed(gain_terms),
+            rowed(width),
             rowed(cols),
             rowed(3 * cols),
             rowed(cols),
@@ -652,11 +668,11 @@
             fixed(taps),
             rowed(keeps.shape[1]),
         ],
-        [lower, upper, pl.BlockSpec((3, 8, cols), lambda i, s, t: (0, 0, 0))] + [any_spec] * 4,
+        [lower, upper, pl.BlockSpec((8, width), lambda i, s, t: (0, 0))] + [any_spec] * 4,
         [
             shape(rows, width),
             shape(rows, width),
-            jax.ShapeDtypeStruct((3, 8, cols), F32),
+            shape(8, width, F32),
         ]
         + [grad] * 4,
         [
@@ -666,16 +682,21 @@
             pltpu.VMEM((tile, 3 * cols), LOW),
             pltpu.VMEM((width, 3 * cols), F32),
             pltpu.VMEM((width, cols), F32),
+            pltpu.VMEM((3, 8, cols), F32),
+            pltpu.VMEM((8, width), F32),
             pltpu.VMEM((2, 2 * chips, width // chips, cols), LOW),
             pltpu.SemaphoreType.DMA((2, 2)),
         ],
         scalars=2,
+        mib=48,
     )(
         idx,
         slots,
         own,
         other,
         edges,
+        x,
+        gain_terms,
         normed_mix,
         mixed,
         parts,
@@ -690,35 +711,25 @@
     )
 
 
-def hidden_back_body(mine_ref, came_ref, x_ref, d_ref, gain_ref, out_ref, sum_ref):
-    step = pl.program_id(0)
+def hidden_back_body(mine_ref, came_ref, x_ref, d_ref, gain_ref, out_ref):
     upstream = mine_ref[...].astype(F32) + came_ref[...].astype(F32)
     resid = x_ref[...].astype(F32)
     scale = lax.rsqrt(jnp.mean(resid * resid, axis=-1, keepdims=True) + EPS)
-    back, terms = norm_back(upstream, resid, scale, gain_ref[...])
-    out_ref[...] = d_ref[...] + back
-    part = jnp.sum(terms.reshape(-1, 8, terms.shape[1]), axis=0)
-
-    @pl.when(step == 0)
-    def _():
-        sum_ref[...] = part
-
-    @pl.when(step > 0)
-    def _():
-        sum_ref[...] += part
+    out_ref[...] = d_ref[...] + norm_back(upstream, resid, scale, gain_ref[...])[0]
 
 
 def hidden_back(mine, came, x, d_resid, gain):
     rows, width = x.shape
-    plain = pl.BlockSpec((TILE, width), lambda i: (i, 0))
+    plain = pl.BlockSpec((TILE // 2, width), lambda i: (i, 0))
     return call(
         hidden_back_body,
         "hidden_back",
-        (rows // TILE,),
+        (2 * rows // TILE,),
         [plain] * 4 + [whole(gain)],
-        [plain, pl.BlockSpec((8, width), lambda i: (0, 0))],
-        [shape(rows, width, F32), shape(8, width, F32)],
+        plain,
+        shape(rows, width, F32),
         scalars=0,
+        mib=12,
     )(mine, came, x, d_resid, gain)
 
 
@@ -731,14 +742,18 @@
     def start(self, send):
         self.terms.append(swap(send, self.links.pop(0)))
 
-    def step(self, *after):
+    def step(self, *after, first=None):
         self.half //= 2
         half = self.half
         terms = self.terms
         if after:
             terms = [tie(terms[0], *after)] + terms[1:]
         going = sum(term[half : 2 * half].astype(F32) for term in terms).astype(LOW)
-        self.terms.append(swap(going, self.links.pop(0)))
+        link = self.links.pop(0)
+        self.terms.append(swap(going, link))
+        if first is not None:
+            first = first + tie(swap(first, link), self.terms[-1])
+        return first
 
     def done(self):
         return sum(term[0].astype(F32) for term in self.terms)
@@ -771,7 +786,7 @@
     half = out_weight.shape[0] // 2
     cols = 2 * half
     place = chip & 3
-    idx = jnp.stack([core, place]).astype(jnp.int32)
+    idx = jnp.stack([core, place, pair]).astype(jnp.int32)
 
     def slots_of(*orders):
         masks = [mask for order in orders for mask in slot_masks(order)]
@@ -795,11 +810,11 @@
         from_out = lax.dynamic_slice(out_weight, (core * half, number * depth), (half, depth))
         return jnp.concatenate([from_in, from_out[None]], axis=0)
 
-    sent_zero = piece(place)
+    small_other = swap_pair(small)
+    sent_zero = tie(piece(place), small)
     sent_three = piece(place ^ 3)
     piece_zero = swap_pair(sent_zero)
     piece_three = swap_pair(sent_three)
-    small_other = swap_pair(tie(small, sent_zero))
     piece_one = swap(piece_zero, 1)
     piece_two = swap(piece_zero, 2)
     far_weights = (piece_zero, piece_one, piece_two, piece_three)
@@ -809,7 +824,7 @@
     other = swap_core(own)
     chip_hidden = jnp.concatenate([own, other], axis=0)
     cot = cotangent.reshape(rows, width)
-    cot_far = swap_pair(tie(cot, piece_zero))
+    cot_far = swap_pair(jnp.concatenate([tie(cot, piece_zero), cot[:16]], axis=0))
 
     seg_low = segments.astype(LOW)
     seg_other = swap_core(seg_low)
@@ -859,16 +874,22 @@
         axis=1,
     ).astype(F32)
 
-    normed_mix, parts, conv_in, conv_out, mixed, mix_part, c_edge = conv_forward(
+    normed_mix, parts, conv_in, conv_out, mixed, mix_own, mix_other, c_edge = conv_forward(
         idx, chip_hidden, edge_rows, in_planes, out_weight, far_weights, gain_mix, taps, keeps, block
     )
-    mix_came = swap_core(mix_part)
-    own_x, resid_two = second_norm(chip_hidden, mix_part, mix_came, gain_ffn, 0, True)
+    mix_to_own = swap_core(mix_other)
+    mix_to_other = swap_core(mix_own)
+    own_x, resid_two = second_norm(
+        tie(chip_hidden, cot_far), mix_own, mix_to_own, gain_ffn, 0, True
+    )
     far_x = swap_pair(own_x)
-    other_x = second_norm(tie(chip_hidden, own_x), mix_part, mix_came, gain_ffn, 1, False)[0]
-
-    cot_other = swap_core(cot)
-    cot_diag = swap_core(tie(cot_far, mix_came))
+    other_x = second_norm(
+        tie(chip_hidden, own_x), mix_other, mix_to_other, gain_ffn, 1, False
+    )[0]
+
+    cot_other = swap_core(tie(cot, piece_zero))
+    cot_far = tie(cot_far, own_x)[:rows]
+    cot_diag = swap_core(cot_far)
     total = 4 * rows
     act, d_gate, d_up, term_own, term_other, d_own, d_other = feed_forward(
         idx, [own_x, other_x], [cot, cot_other], weights, total, 0, ()
@@ -897,15 +918,13 @@
     term_home = swap_pair(
         (term_far.astype(F32) + swap_core(tie(term_diag, down_send)).astype(F32)).astype(LOW)
     )
-    gate_send, gate_keep, up_send, up_keep = weight_grads(
-        slots_of(turned, links), chips, [own_x, other_x, far_x, diag_x], [d_gate, tie(d_up, down_send)]
-    )
-    sum_gate = Halving(gate_keep, turned)
-    sum_gate.start(gate_send)
-    sum_up = Halving(up_keep, links)
-    sum_up.start(up_send)
-
-    d_resid, d_low, gain_ffn_terms = resid_back(d_own, near_d, home, resid_two, cot, gain_ffn)
+    xs = [own_x, other_x, far_x, diag_x]
+    gate_send, gate_keep = weight_grads(slots_of(turned), chips, xs, [tie(d_gate, down_send)])
+    up_send, up_keep = weight_grads(slots_of(links), chips, xs, [tie(d_up, gate_send)])
+
+    d_resid, d_low, gain_ffn_terms = resid_back(
+        d_own, near_d, home, tie(resid_two, up_send), cot, gain_ffn
+    )
     d_near = swap_core(d_low)
     d_head = d_low.reshape(groups, block, width)[:, :2]
     d_after = jnp.where(
@@ -913,6 +932,10 @@
         over_seq(d_head, [(i, i - 2) for i in even]),
         over_seq(d_head, [(i, i - 1) for i in even]),
     )
+    sum_gate = Halving(gate_keep, turned)
+    sum_gate.start(tie(gate_send, d_head))
+    sum_up = Halving(up_keep, links)
+    sum_up.start(tie(up_send, d_head))
     d_edges = after_blocks(
         d_after, d_head, d_near.reshape(groups, block, width)[:, :2]
     ).reshape(4 * groups, width)
@@ -921,13 +944,15 @@
     slots_mix = slots_of(
         *[[0 if link == "pair" else link for link in order] for order in orders]
     )
-    d_normed_own, d_normed_other, tap_terms, send_a, keep_a, send_b, keep_b = conv_back(
+    d_normed_own, d_normed_other, sums, send_a, keep_a, send_b, keep_b = conv_back(
         idx,
         slots_mix,
         chips,
         d_low,
         d_near,
         d_edges,
+        chip_hidden,
+        gain_ffn_terms,
         (normed_mix, parts, conv_in, conv_out, mixed, c_edge),
         in_planes,
         out_weight,
@@ -940,41 +965,21 @@
     sum_b = Halving(keep_b, orders[1])
     sum_a.start(send_a)
     sum_b.start(send_b)
+    sums = sums + tie(swap_pair(sums), sum_a.terms[-1])
     d_normed_came = swap_core(d_normed_other)
     sum_gate.step(send_a)
     sum_up.step(send_a)
     sum_down.step(send_a)
-    grad_hidden, gain_mix_terms = hidden_back(
-        d_normed_own, d_normed_came, own, d_resid, gain_mix
-    )
-
-    taps_sum = jnp.sum(tap_terms, axis=1)
-    half_width = norm_mix.shape[0]
-    spread = jnp.zeros((3, width), F32)
-    spread = lax.dynamic_update_slice_in_dim(
-        spread, taps_sum[:, :half], pair * half_width + core * half, 1
-    )
-    spread = lax.dynamic_update_slice_in_dim(
-        spread, taps_sum[:, half:], (1 - pair) * half_width + core * half, 1
-    )
-    sums = jnp.concatenate(
-        [
-            spread,
-            jnp.sum(gain_mix_terms, axis=0, keepdims=True),
-            jnp.sum(gain_ffn_terms, axis=0, keepdims=True),
-        ],
-        axis=0,
-    )
-    sums = sums + swap_core(sums)
-    for link in ["pair"] + links:
-        sums = sums + swap(sums, link)
-    sums = lax.dynamic_slice_in_dim(sums, pair * half_width, half_width, 1)
+    grad_hidden = hidden_back(d_normed_own, d_normed_came, own, d_resid, gain_mix)
     for reduction in (sum_down, sum_gate, sum_up):
         while reduction.links:
             reduction.step(grad_hidden)
     while sum_a.links:
-        sum_a.step()
+        sums = sum_a.step(first=sums)
         sum_b.step()
+    sums = sums + swap_core(sums)
+    half_width = norm_mix.shape[0]
+    sums = lax.dynamic_slice_in_dim(sums, pair * half_width, half_width, 1)
 
     block_out = (
         resid_two

time: 369 us -> 313 us (0.85)
  Pallas kernels: 154 us -> 114 us
  other arithmetic: 43.8 us -> 27.2 us
  local copies, waits for them, and re-layouts: 15.4 us -> 23.9 us
  starting transfers between devices: 53.2 us -> 46.8 us
    ppermute x10, waiting for transfers between devices: 33.7 us -> 9.85 us  [swap_pair(): return lax.ppermute(block, 'wshard', [(0, 1), (1, 0)])]
    ppermute x39 -> x40, waiting for transfers between devices: 64.3 us -> 85.3 us  [over_seq(): return lax.ppermute(block, 'seq', route)]
    pallas_call x2, Pallas kernels: 66.1 us -> 45.6 us  [feed_forward(): call(functools.partial(feed_forward_body, count, len(held)), 'feed_forwar...]
    unnamed x64 -> x100, local copies, waits for them, and re-layouts: 4.6 us -> 15.3 us
    pallas_call x2 -> x3, Pallas kernels: 36.8 us -> 26.8 us  [weight_grads(): call(functools.partial(grads_body, pieces, count, chips), 'weight_grads',...]
    convert_element_type x12, other arithmetic: 14.4 us -> 6.35 us  [step(): going = sum((term[half:2 * half].astype(F32) for term in terms)).astype(LOW)]
    pallas_call x3, Pallas kernels: 12.9 us -> 5.46 us  [the longest x2 3.02 us: second_norm(): call(second_norm_body, 'second_norm', (4,), [plain(which), plain(0), plai...]
    reduce_sum x3 -> x0, other arithmetic: 4.14 us -> none  [the longest x1 1.42 us: local(): taps_sum = jnp.sum(tap_terms, axis=1)]
  transfers between devices with their start and end apart: 49 -> 50, of which waited for: 16 -> 19; matrix products, arithmetic and copies ran while one was open for 14% -> 10% of each run, Pallas kernels for 28% -> 30%
where the time goes in v3:
time: 313 us; the launch traced here: 309 us
  Pallas kernels  114 us (36%)
  waiting for transfers between devices  95.2 us (30%)
  starting transfers between devices  46.8 us (15%)
  other arithmetic  27.2 us (9%)
  local copies, waits for them, and re-layouts  23.9 us (8%)
    ppermute x40, waiting for transfers between devices, over_seq(): return lax.ppermute(block, 'seq', route)  85.3 us
    pallas_call x2, Pallas kernels, feed_forward(): call(functools.partial(feed_forward_body, count, len(held)), 'feed_forwar...  45.6 us
    ppermute x40, starting transfers between devices, over_seq(): return lax.ppermute(block, 'seq', route)  36.4 us
    pallas_call x3, Pallas kernels, weight_grads(): call(functools.partial(grads_body, pieces, count, chips), 'weight_grads',...  26.8 us
    pallas_call x1, Pallas kernels, conv_back(): call(functools.partial(conv_back_body, block, count, chips), 'conv_back',...  20.4 us
    unnamed x100, local copies, waits for them, and re-layouts  15.3 us
    pallas_call x1, Pallas kernels, conv_forward(): call(functools.partial(conv_forward_body, block), 'conv_forward', (total...  12.9 us
    ppermute x10, starting transfers between devices, swap_pair(): return lax.ppermute(block, 'wshard', [(0, 1), (1, 0)])  10.3 us
  transfers between devices with their start and end apart: 50, of which 19 were waited for; matrix products, arithmetic and copies ran while one was open for 10% of the time, Pallas kernels for 30%

profile of v3, /device:TPU:0, one launch (start us, length us, event | category | flops | bytes accessed | tf_op | source)
XLA Modules:
  0.0 309.3 jit_solution(15059598503215375416)
XLA Ops:
  2.7 3.0 collective-permute-start.9
  14.3 9.8 %collective-permute-done.1.r0 = bf16[4,256,256]{2,1,0:T(8,128)(2,1)} collective-permute-done((bf16[4,256,256]{2,1,0:T(8,128)(2,1)}, bf16[4,256,256]{2,1,0:T(8,128)(2,1)}, u32[]{:S(2)}, u32[]{:S(2)}) %collective-permute-start.1) | collective-permute-done | bytes 524320 | tf_op jit(solution)/shard_map/ppermute | solution.py:31
  37.7 4.5 %collective-permute-done.5 = bf16[4,2,1152]{2,1,0:T(2,128)(2,1)S(1)} collective-permute-done((bf16[4,2,1152]{2,1,0:T(2,128)(2,1)S(1)}, bf16[4,2,1152]{2,1,0:T(2,128)(2,1)S(1)}, u32[]{:S(2)}, u32[]{:S(2)}) %collective-permute-start.5) | collective-permute-done | bytes 18464 | tf_op jit(solution)/shard_map/ppermute | solution.py:19
  46.5 12.9 %conv_forward.1 = (bf16[1024,1024]{1,0:T(8,128)(2,1)}, bf16[1024,1536]{1,0:T(8,128)(2,1)}, bf16[1024,512]{1,0:T(8,128)(2,1)}, bf16[1024,512]{1,0:T(8,128)(2,1)},...) custom-call(s32[3]{0:T(128)S(1)} %pad_add_fusion.1.idx, ...), custom_call_target="tpu_custom_call" | custom-call | flops 1000 | bytes 1000 | tf_op jit(solution)/shard_map/conv_forward/pallas_call | solution.py:208
  68.1 22.8 %feed_forward.2 = (bf16[2048,1152]{1,0:T(8,128)(2,1)S(1)}, bf16[2048,1152]{1,0:T(8,128)(2,1)S(1)}, bf16[2048,1152]{1,0:T(8,128)(2,1)S(1)}, bf16[512,1024]{1,0:T(...) custom-call(s32[3]{0:T(128)S(1)} %pad_add_fusion.1.idx, ...), custom_call_target="tpu_custom_call" | custom-call | flops 1000 | bytes 1000 | tf_op jit(solution)/shard_map/feed_forward/pallas_call | solution.py:328
  94.7 22.9 %feed_forward.3 = (bf16[2048,1152]{1,0:T(8,128)(2,1)S(1)}, bf16[2048,1152]{1,0:T(8,128)(2,1)S(1)}, bf16[2048,1152]{1,0:T(8,128)(2,1)S(1)}, bf16[512,1024]{1,0:T(...) custom-call(s32[3]{0:T(128)S(1)} %pad_add_fusion.1.idx, ...), custom_call_target="tpu_custom_call", output_to_operand_aliasing={{0}: (8, {}), {1}: (9, {}), {2}: (10, {})} | custom-call | flops 1000 | bytes 1000 | tf_op jit(solution)/shard_map/feed_forward/pallas_call | solution.py:328
  120.4 9.0 %weight_grads.3 = (bf16[4,128,1152]{2,1,0:T(8,128)(2,1)}, bf16[4,128,1152]{2,1,0:T(8,128)(2,1)S(1)}) custom-call(s32[8]{0:T(128)S(1)} %broadcast_xor_fusion.2.slots, bf16[512,1024]{1,0:T(8,128)(2,1)S(1)} %bitcast.74, bf16[512,1024]{1,0:T(8,128)(2,1)S(1)} %collective-permute-done.12.refs_3_.refs_1_, bf16[512,1024]{1,0:T(8,128)(2,1)S(1)} %slice.329.refs_2_, ...), custom_call_target="tpu_custom_call" | custom-call | flops 1000 | bytes 1000 | tf_op jit(solution)/shard_map/weight_grads/pallas_call | solution.py:401
  132.5 2.9 collective-permute-start.35
  141.6 8.9 %weight_grads.4 = (bf16[4,128,1152]{2,1,0:T(8,128)(2,1)}, bf16[4,128,1152]{2,1,0:T(8,128)(2,1)S(1)}) custom-call(s32[8]{0:T(128)S(1)} %broadcast_xor_fusion.1.slots, bf16[512,1024]{1,0:T(8,128)(2,1)S(1)} %copy-done.13, bf16[512,1024]{1,0:T(8,128)(2,1)S(1)} %copy-done.6, bf16[512,1024]{1,0:T(8,128)(2,1)S(1)} %copy-done.9, bf16[512,1024]{1,0:T(8,128)(2,1)S(1)} %copy-done.11, ...), custom_call_target="tpu_custom_call" | custom-call | flops 1000 | bytes 1000 | tf_op jit(solution)/shard_map/weight_grads/pallas_call | solution.py:401
  151.5 9.0 %weight_grads.5 = (bf16[4,128,1152]{2,1,0:T(8,128)(2,1)}, bf16[4,128,1152]{2,1,0:T(8,128)(2,1)S(1)}) custom-call(s32[8]{0:T(128)S(1)} %broadcast_xor_fusion.2.slots, bf16[512,1024]{1,0:T(8,128)(2,1)S(1)} %copy-done.13, bf16[512,1024]{1,0:T(8,128)(2,1)S(1)} %copy-done.6, bf16[512,1024]{1,0:T(8,128)(2,1)S(1)} %copy-done.9, bf16[512,1024]{1,0:T(8,128)(2,1)S(1)} %copy-done.11, ...), custom_call_target="tpu_custom_call" | custom-call | flops 1000 | bytes 1000 | tf_op jit(solution)/shard_map/weight_grads/pallas_call | solution.py:401
  160.6 3.1 resid_back.1
  164.1 3.7 %add_convert_fusion.2 = bf16[512,1024]{1,0:T(8,128)(2,1)} fusion(bf16[512,1024]{1,0:T(8,128)(2,1)} %collective-permute-done.17, bf16[512,1024]{1,0:T(8,128)(2,1)S(1)} %copy-done.31), kind=kLoop, calls=%fused_computation.3 | loop fusion | flops 2097152 | bytes 3145728 | tf_op jit(solution)/shard_map/convert_element_type | solution.py:919
  179.5 20.4 %conv_back.1 = (bf16[512,1024]{1,0:T(8,128)(2,1)S(1)}, bf16[512,1024]{1,0:T(8,128)(2,1)S(1)}, f32[8,1024]{1,0:T(8,128)S(1)}, bf16[8,128,512]{2,1,0:T(8,128)(2,1)...) custom-call(s32[3]{0:T(128)S(1)} %pad_add_fusion.1.idx, ...), custom_call_target="tpu_custom_call" | custom-call | flops 1000 | bytes 1000 | tf_op jit(solution)/shard_map/conv_back/pallas_call | solution.py:649
  200.5 3.4 %add_convert_fusion = bf16[512,1024]{1,0:T(8,128)(2,1)} fusion(f32[512,1024]{1,0:T(8,128)S(1)} %copy-done.15, bf16[512,1024]{1,0:T(8,128)(2,1)} %collective-permute-done.18, bf16[512,1024]{1,0:T(8,128)(2,1)} %collective-permute-done.13, bf16[512,1024]{1,0:T(8,128)(2,1)S(1)} %copy-done.33), kind=kLoop, calls=%fused_computation.1 | loop fusion | flops 3670016 | bytes 6291456 | tf_op jit(solution)/shard_map/convert_element_type | solution.py:987
  203.9 13.5 %collective-permute-done.36 = bf16[2,128,1152]{2,1,0:T(8,128)(2,1)} collective-permute-done((bf16[2,128,1152]{2,1,0:T(8,128)(2,1)}, bf16[2,128,1152]{2,1,0:T(8,128)(2,1)}, u32[]{:S(2)}, u32[]{:S(2)}) %collective-permute-start.36) | collective-permute-done | bytes 589856 | tf_op jit(solution)/shard_map/ppermute | solution.py:19
  224.0 11.6 %collective-permute-done.37 = bf16[1,128,1152]{2,1,0:T(8,128)(2,1)S(1)} collective-permute-done((bf16[1,128,1152]{2,1,0:T(8,128)(2,1)S(1)}, bf16[1,128,1152]{2,1,0:T(8,128)(2,1)S(1)}, u32[]{:S(2)}, u32[]{:S(2)}) %collective-permute-start.37) | collective-permute-done | bytes 294944 | tf_op jit(solution)/shard_map/ppermute | solution.py:19
  239.6 3.9 %collective-permute-done.30 = bf16[8,128,512]{2,1,0:T(8,128)(2,1)S(1)} collective-permute-done((bf16[8,128,512]{2,1,0:T(8,128)(2,1)S(1)}, bf16[8,128,512]{2,1,0:T(8,128)(2,1)S(1)}, u32[]{:S(2)}, u32[]{:S(2)}) %collective-permute-start.30) | collective-permute-done | bytes 1048608 | tf_op jit(solution)/shard_map/ppermute | solution.py:19
  245.6 3.9 %collective-permute-done.42 = bf16[2,128,1152]{2,1,0:T(8,128)(2,1)S(1)} collective-permute-done((bf16[2,128,1152]{2,1,0:T(8,128)(2,1)S(1)}, bf16[2,128,1152]{2,1,0:T(8,128)(2,1)S(1)}, u32[]{:S(2)}, u32[]{:S(2)}) %collective-permute-start.42) | collective-permute-done | bytes 589856 | tf_op jit(solution)/shard_map/ppermute | solution.py:19
  251.9 4.2 %collective-permute-done.39 = bf16[2,128,1152]{2,1,0:T(8,128)(2,1)S(1)} collective-permute-done((bf16[2,128,1152]{2,1,0:T(8,128)(2,1)S(1)}, bf16[2,128,1152]{2,1,0:T(8,128)(2,1)S(1)}, u32[]{:S(2)}, u32[]{:S(2)}) %collective-permute-start.39) | collective-permute-done | bytes 589856 | tf_op jit(solution)/shard_map/ppermute | solution.py:19
  259.7 11.8 %collective-permute-done.43 = bf16[1,128,1152]{2,1,0:T(8,128)(2,1)S(1)} collective-permute-done((bf16[1,128,1152]{2,1,0:T(8,128)(2,1)S(1)}, bf16[1,128,1152]{2,1,0:T(8,128)(2,1)S(1)}, u32[]{:S(2)}, u32[]{:S(2)}) %collective-permute-start.43) | collective-permute-done | bytes 294944 | tf_op jit(solution)/shard_map/ppermute | solution.py:19
  272.7 4.5 %collective-permute-done.40 = bf16[1,128,1152]{2,1,0:T(8,128)(2,1)S(1)} collective-permute-done((bf16[1,128,1152]{2,1,0:T(8,128)(2,1)S(1)}, bf16[1,128,1152]{2,1,0:T(8,128)(2,1)S(1)}, u32[]{:S(2)}, u32[]{:S(2)}) %collective-permute-start.40) | collective-permute-done | bytes 294944 | tf_op jit(solution)/shard_map/ppermute | solution.py:19
  282.7 4.5 %collective-permute-done.32 = bf16[2,128,512]{2,1,0:T(8,128)(2,1)S(1)} collective-permute-done((bf16[2,128,512]{2,1,0:T(8,128)(2,1)S(1)}, bf16[2,128,512]{2,1,0:T(8,128)(2,1)S(1)}, u32[]{:S(2)}, u32[]{:S(2)}) %collective-permute-start.32) | collective-permute-done | bytes 262176 | tf_op jit(solution)/shard_map/ppermute | solution.py:19
  289.0 6.5 %collective-permute-done.28 = bf16[2,128,512]{2,1,0:T(8,128)(2,1)S(1)} collective-permute-done((bf16[2,128,512]{2,1,0:T(8,128)(2,1)S(1)}, bf16[2,128,512]{2,1,0:T(8,128)(2,1)S(1)}, u32[]{:S(2)}, u32[]{:S(2)}) %collective-permute-start.28) | collective-permute-done | bytes 262176 | tf_op jit(solution)/shard_map/ppermute | solution.py:19
  298.7 5.7 %collective-permute-done.29 = bf16[1,128,512]{2,1,0:T(8,128)(2,1)S(1)} collective-permute-done((bf16[1,128,512]{2,1,0:T(8,128)(2,1)S(1)}, bf16[1,128,512]{2,1,0:T(8,128)(2,1)S(1)}, u32[]{:S(2)}, u32[]{:S(2)}) %collective-permute-start.29) | collective-permute-done | bytes 131104 | tf_op jit(solution)/shard_map/ppermute | solution.py:19
  (290 shorter events, 101.2 us)
Async XLA Ops:
  9.9 33.3 %collective-permute-start.8 = (bf16[4,256,256]{2,1,0:T(8,128)(2,1)}, bf16[4,256,256]{2,1,0:T(8,128)(2,1)}, u32[]{:S(2)}, u32[]{:S(2)}) collective-permute-start(bf16[4,256,256]{2,1,0:T(8,128)(2,1)} %pad_maximum_fusion.4), channel_id=1, source_target_pairs={{0,1},{1,0},{2,3},{3,2},{4,5},{5,4},{6,7},{7,6},{8,9},{9,8},{10,11... | collective-permute-start | bytes 1572872 | tf_op jit(solution)/shard_map/ppermute | solution.py:31
  25.2 34.8 %collective-permute-start.2 = (bf16[528,1024]{1,0:T(8,128)(2,1)}, bf16[528,1024]{1,0:T(8,128)(2,1)}, u32[]{:S(2)}, u32[]{:S(2)}) collective-permute-start(bf16[528,1024]{1,0:T(8,128)(2,1)} %pad_maximum_fusion.2), channel_id=1, source_target_pairs={{0,1},{1,0},{2,3},{3,2},{4,5},{5,4},{6,7},{7,6},{8,9},{9,8},{10,11... | collective-permute-start | bytes 3244040 | tf_op jit(solution)/shard_map/ppermute | solution.py:31
  25.2 18.0 %collective-permute-start.6 = (bf16[4,256,256]{2,1,0:T(8,128)(2,1)}, bf16[4,256,256]{2,1,0:T(8,128)(2,1)}, u32[]{:S(2)}, u32[]{:S(2)}) collective-permute-start(bf16[4,256,256]{2,1,0:T(8,128)(2,1)} %collective-permute-done.1.r0), channel_id=1, source_target_pairs={{0,4},{2,6},{4,0},{6,2},{8,12},{10,14},{12,8},{14,10},{16,20},{18,... | collective-permute-start | bytes 1572872 | tf_op jit(solution)/shard_map/ppermute | solution.py:19
  64.2 27.7 %collective-permute-start.14 = (bf16[512,1024]{1,0:T(8,128)(2,1)S(1)}, bf16[512,1024]{1,0:T(8,128)(2,1)S(1)}, u32[]{:S(2)}, u32[]{:S(2)}) collective-permute-start(bf16[512,1024]{1,0:T(8,128)(2,1)S(1)} %get-tuple-element.84.refs_0_), channel_id=1, source_target_pairs={{0,1},{1,0},{2,3},{3,2},{4,5},{5,4},{6,7},{7,6},{8,9},{9,8},{10,11... | collective-permute-start | bytes 3145736 | tf_op jit(solution)/shard_map/ppermute | solution.py:31
  67.0 25.4 %collective-permute-start.16 = (bf16[512,1024]{1,0:T(8,128)(2,1)S(1)}, bf16[512,1024]{1,0:T(8,128)(2,1)S(1)}, u32[]{:S(2)}, u32[]{:S(2)}) collective-permute-start(bf16[512,1024]{1,0:T(8,128)(2,1)S(1)} %slice.329.refs_2_), channel_id=1, source_target_pairs={{0,2},{2,0},{4,6},{6,4},{8,10},{10,8},{12,14},{14,12},{16,18},{18,... | collective-permute-start | bytes 3145736 | tf_op jit(solution)/shard_map/ppermute | solution.py:19
  120.3 40.3 %collective-permute-start.19 = (bf16[512,1024]{1,0:T(8,128)(2,1)}, bf16[512,1024]{1,0:T(8,128)(2,1)}, u32[]{:S(2)}, u32[]{:S(2)}) collective-permute-start(bf16[512,1024]{1,0:T(8,128)(2,1)} %get-tuple-element.99), channel_id=1, source_target_pairs={{0,2},{2,0},{4,6},{6,4},{8,10},{10,8},{12,14},{14,12},{16,18},{18,... | collective-permute-start | bytes 3145736 | tf_op jit(solution)/shard_map/ppermute | solution.py:19
  131.9 28.6 %collective-permute-start.21 = (bf16[512,1024]{1,0:T(8,128)(2,1)}, bf16[512,1024]{1,0:T(8,128)(2,1)}, u32[]{:S(2)}, u32[]{:S(2)}) collective-permute-start(bf16[512,1024]{1,0:T(8,128)(2,1)} %add_convert_fusion.1), channel_id=1, source_target_pairs={{0,1},{1,0},{2,3},{3,2},{4,5},{5,4},{6,7},{7,6},{8,9},{9,8},{10,11... | collective-permute-start | bytes 3145736 | tf_op jit(solution)/shard_map/ppermute | solution.py:31
  132.4 31.7 %collective-permute-start.17 = (bf16[512,1024]{1,0:T(8,128)(2,1)}, bf16[512,1024]{1,0:T(8,128)(2,1)}, u32[]{:S(2)}, u32[]{:S(2)}) collective-permute-start(bf16[512,1024]{1,0:T(8,128)(2,1)} %get-tuple-element.98), channel_id=1, source_target_pairs={{0,2},{2,0},{4,6},{6,4},{8,10},{10,8},{12,14},{14,12},{16,18},{18,... | collective-permute-start | bytes 3145736 | tf_op jit(solution)/shard_map/ppermute | solution.py:19
  132.5 38.2 %collective-permute-start.35 = (bf16[4,128,1152]{2,1,0:T(8,128)(2,1)}, bf16[4,128,1152]{2,1,0:T(8,128)(2,1)}, u32[]{:S(2)}, u32[]{:S(2)}) collective-permute-start(bf16[4,128,1152]{2,1,0:T(8,128)(2,1)} %get-tuple-element.97), channel_id=1, source_target_pairs={{0,4},{2,6},{4,0},{6,2},{8,12},{10,14},{12,8},{14,10},{16,20},{18,... | collective-permute-start | bytes 3538952 | tf_op jit(solution)/shard_map/ppermute | solution.py:19
  135.4 65.1 %collective-permute-start.13 = (bf16[512,1024]{1,0:T(8,128)(2,1)}, bf16[512,1024]{1,0:T(8,128)(2,1)}, u32[]{:S(2)}, u32[]{:S(2)}) collective-permute-start(bf16[512,1024]{1,0:T(8,128)(2,1)} %copy-done.36), channel_id=1, source_target_pairs={{0,2},{2,0},{4,6},{6,4},{8,10},{10,8},{12,14},{14,12},{16,18},{18,... | collective-permute-start | bytes 3145736 | tf_op jit(solution)/shard_map/ppermute | solution.py:19
  167.8 32.1 %collective-permute-start.18 = (bf16[512,1024]{1,0:T(8,128)(2,1)}, bf16[512,1024]{1,0:T(8,128)(2,1)}, u32[]{:S(2)}, u32[]{:S(2)}) collective-permute-start(bf16[512,1024]{1,0:T(8,128)(2,1)} %add_convert_fusion.2), channel_id=1, source_target_pairs={{0,1},{1,0},{2,3},{3,2},{4,5},{5,4},{6,7},{7,6},{8,9},{9,8},{10,11... | collective-permute-start | bytes 3145736 | tf_op jit(solution)/shard_map/ppermute | solution.py:31
  175.0 44.8 %collective-permute-start.41 = (bf16[4,128,1152]{2,1,0:T(8,128)(2,1)}, bf16[4,128,1152]{2,1,0:T(8,128)(2,1)}, u32[]{:S(2)}, u32[]{:S(2)}) collective-permute-start(bf16[4,128,1152]{2,1,0:T(8,128)(2,1)} %get-tuple-element.134), channel_id=1, source_target_pairs={{0,4},{2,6},{4,0},{6,2},{8,12},{10,14},{12,8},{14,10},{16,20},{18,... | collective-permute-start | bytes 3538952 | tf_op jit(solution)/shard_map/ppermute | solution.py:19
  176.7 46.5 %collective-permute-start.38 = (bf16[4,128,1152]{2,1,0:T(8,128)(2,1)}, bf16[4,128,1152]{2,1,0:T(8,128)(2,1)S(1)}, u32[]{:S(2)}, u32[]{:S(2)}) collective-permute-start(bf16[4,128,1152]{2,1,0:T(8,128)(2,1)} %get-tuple-element.130), channel_id=1, source_target_pairs={{0,8},{2,10},{4,12},{6,14},{8,0},{10,2},{12,4},{14,6},{16,24},{18,... | collective-permute-start | bytes 3538952 | tf_op jit(solution)/shard_map/ppermute | solution.py:19
  178.3 39.0 %collective-permute-start.36 = (bf16[2,128,1152]{2,1,0:T(8,128)(2,1)}, bf16[2,128,1152]{2,1,0:T(8,128)(2,1)}, u32[]{:S(2)}, u32[]{:S(2)}) collective-permute-start(bf16[2,128,1152]{2,1,0:T(8,128)(2,1)} %add_convert_fusion.5), channel_id=1, source_target_pairs={{0,8},{2,10},{4,12},{6,14},{8,0},{10,2},{12,4},{14,6},{16,24},{18,... | collective-permute-start | bytes 1769480 | tf_op jit(solution)/shard_map/ppermute | solution.py:19
  199.9 44.3 %collective-permute-start.26 = (bf16[8,128,512]{2,1,0:T(8,128)(2,1)S(1)}, bf16[8,128,512]{2,1,0:T(8,128)(2,1)S(1)}, u32[]{:S(2)}, u32[]{:S(2)}) collective-permute-start(bf16[8,128,512]{2,1,0:T(8,128)(2,1)S(1)} %get-tuple-element.118), channel_id=1, source_target_pairs={{0,1},{1,0},{2,3},{3,2},{4,5},{5,4},{6,7},{7,6},{8,9},{9,8},{10,11... | collective-permute-start | bytes 3145736 | tf_op jit(solution)/shard_map/ppermute | solution.py:31
  203.9 32.9 %collective-permute-start.25 = (bf16[512,1024]{1,0:T(8,128)(2,1)S(1)}, bf16[512,1024]{1,0:T(8,128)(2,1)S(1)}, u32[]{:S(2)}, u32[]{:S(2)}) collective-permute-start(bf16[512,1024]{1,0:T(8,128)(2,1)S(1)} %get-tuple-element.121), channel_id=1, source_target_pairs={{0,2},{2,0},{4,6},{6,4},{8,10},{10,8},{12,14},{14,12},{16,18},{18,... | collective-permute-start | bytes 3145736 | tf_op jit(solution)/shard_map/ppermute | solution.py:19
  217.4 26.1 %collective-permute-start.30 = (bf16[8,128,512]{2,1,0:T(8,128)(2,1)S(1)}, bf16[8,128,512]{2,1,0:T(8,128)(2,1)S(1)}, u32[]{:S(2)}, u32[]{:S(2)}) collective-permute-start(bf16[8,128,512]{2,1,0:T(8,128)(2,1)S(1)} %copy-done.44), channel_id=1, source_target_pairs={{0,4},{2,6},{4,0},{6,2},{8,12},{10,14},{12,8},{14,10},{16,20},{18,... | collective-permute-start | bytes 3145736 | tf_op jit(solution)/shard_map/ppermute | solution.py:19
  223.2 35.6 %collective-permute-start.45 = (f32[8,1024]{1,0:T(8,128)S(1)}, f32[8,1024]{1,0:T(8,128)S(1)}, u32[]{:S(2)}, u32[]{:S(2)}) collective-permute-start(f32[8,1024]{1,0:T(8,128)S(1)} %get-tuple-element.137), channel_id=1, source_target_pairs={{0,1},{1,0},{2,3},{3,2},{4,5},{5,4},{6,7},{7,6},{8,9},{9,8},{10,11... | collective-permute-start | bytes 98312 | tf_op jit(solution)/shard_map/ppermute | solution.py:31
  236.8 19.3 %collective-permute-start.39 = (bf16[2,128,1152]{2,1,0:T(8,128)(2,1)S(1)}, bf16[2,128,1152]{2,1,0:T(8,128)(2,1)S(1)}, u32[]{:S(2)}, u32[]{:S(2)}) collective-permute-start(bf16[2,128,1152]{2,1,0:T(8,128)(2,1)S(1)} %add_convert_fusion.4), channel_id=1, source_target_pairs={{0,4},{2,6},{4,0},{6,2},{8,12},{10,14},{12,8},{14,10},{16,20},{18,... | collective-permute-start | bytes 1769480 | tf_op jit(solution)/shard_map/ppermute | solution.py:19
  243.6 34.2 %collective-permute-start.31 = (bf16[4,128,512]{2,1,0:T(8,128)(2,1)S(1)}, bf16[4,128,512]{2,1,0:T(8,128)(2,1)S(1)}, u32[]{:S(2)}, u32[]{:S(2)}) collective-permute-start(bf16[4,128,512]{2,1,0:T(8,128)(2,1)S(1)} %add_convert_fusion.6), channel_id=1, source_target_pairs={{0,1},{1,0},{2,3},{3,2},{4,5},{5,4},{6,7},{7,6},{8,9},{9,8},{10,11... | collective-permute-start | bytes 1572872 | tf_op jit(solution)/shard_map/ppermute | solution.py:31
  244.3 34.0 %collective-permute-start.27 = (bf16[4,128,512]{2,1,0:T(8,128)(2,1)S(1)}, bf16[4,128,512]{2,1,0:T(8,128)(2,1)S(1)}, u32[]{:S(2)}, u32[]{:S(2)}) collective-permute-start(bf16[4,128,512]{2,1,0:T(8,128)(2,1)S(1)} %add_convert_fusion.7), channel_id=1, source_target_pairs={{0,4},{2,6},{4,0},{6,2},{8,12},{10,14},{12,8},{14,10},{16,20},{18,... | collective-permute-start | bytes 1572872 | tf_op jit(solution)/shard_map/ppermute | solution.py:19
  250.6 21.0 %collective-permute-start.43 = (bf16[1,128,1152]{2,1,0:T(8,128)(2,1)S(1)}, bf16[1,128,1152]{2,1,0:T(8,128)(2,1)S(1)}, u32[]{:S(2)}, u32[]{:S(2)}) collective-permute-start(bf16[1,128,1152]{2,1,0:T(8,128)(2,1)S(1)} %add_convert_fusion.8), channel_id=1, source_target_pairs={{0,16},{2,18},{4,20},{6,22},{8,24},{10,26},{12,28},{14,30},{16,0},... | collective-permute-start | bytes 884744 | tf_op jit(solution)/shard_map/ppermute | solution.py:19
  256.2 21.0 %collective-permute-start.40 = (bf16[1,128,1152]{2,1,0:T(8,128)(2,1)S(1)}, bf16[1,128,1152]{2,1,0:T(8,128)(2,1)S(1)}, u32[]{:S(2)}, u32[]{:S(2)}) collective-permute-start(bf16[1,128,1152]{2,1,0:T(8,128)(2,1)S(1)} %add_convert_fusion.9), channel_id=1, source_target_pairs={{0,16},{2,18},{4,20},{6,22},{8,24},{10,26},{12,28},{14,30},{16,0},... | collective-permute-start | bytes 884744 | tf_op jit(solution)/shard_map/ppermute | solution.py:19
  258.9 21.3 %collective-permute-start.46 = (f32[8,1024]{1,0:T(8,128)S(1)}, f32[8,1024]{1,0:T(8,128)S(1)}, u32[]{:S(2)}, u32[]{:S(2)}) collective-permute-start(f32[8,1024]{1,0:T(8,128)S(1)} %add.245), channel_id=1, source_target_pairs={{0,4},{2,6},{4,0},{6,2},{8,12},{10,14},{12,8},{14,10},{16,20},{18,... | collective-permute-start | bytes 98312 | tf_op jit(solution)/shard_map/ppermute | solution.py:19
  (76 other events, 771.5 us)
